TPU v7x, 512 devices: a whole 4x4x16 slice. The times are simulated.
512 devices in a mesh: block: 32 (over z_lo, y, core), row: 16 (over x, z_hi).
Axes of the slice: x: 4, y: 4, z: 16 (z_hi: 4, z_lo: 4; z = z_hi * 4 + z_lo), core: 2. Of those that a mesh axis runs over, the one named last changes fastest.
Arguments:
- embed: float32 [196608, 128], P(('block', 'row'))
- partner: int32 [196608], P(('block', 'row')), may hold values from 0 to 6143, as said below
- plan: int32 [2, 32], replicated, may hold values from 0 to 31, as said below
Outputs:
- grad: float32 [196608, 128], P(('block', 'row'))
- log_partition: float32 [196608], P(('block', 'row'))
- loss: float32 [], replicated
Inputs may be any that keep to these rules, and one draw needn't show every extreme that they name: The pairing is mutual within each block: the partner of the partner of a view is the view itself, and no view is its own partner. `plan`: each row pairs all 32 blocks: entry b names the opponent of block b, the opponent's entry names b, no entry names its own block, and no two blocks meet in two rows.
All inputs are finite; a program needn't handle non-finite values.
Results may differ from a plain program's by a relative error of at most 0.0025.
The roundings to bfloat16 on the way count: a program that leaves them out, or rounds other values in their place, can miss the bound.
Values may be sent and summed in bfloat16 or wider, within the bound.
No kernel may reach another device: no remote copies, remote signals or barrier semaphores. Data moves between devices by JAX's collectives and lax.ppermute only.
A program may use at most 128 MiB of HBM per device.

v0:
```python
import jax
import jax.numpy as jnp
from jax import lax
from jax.sharding import PartitionSpec as P

ROUNDS = 2


inverse_tau = 10.0


def fetch_partner(shards):
    return lax.all_gather(shards, "row", axis=1, tiled=True)


def exp_rows(anchor_embeddings, candidate_embeddings):
    similarity_grid = (
        jnp.einsum(
            "qe,ke->qk", anchor_embeddings, candidate_embeddings, preferred_element_type=jnp.float32
        )
        * inverse_tau
    )
    return (similarity_grid, jnp.exp(similarity_grid - inverse_tau))


def weighted_keys(anchor_embeddings, candidate_embeddings, query_lse, key_lse, self_mask):
    similarity_grid = (
        jnp.einsum(
            "qe,ke->qk", anchor_embeddings, candidate_embeddings, preferred_element_type=jnp.float32
        )
        * inverse_tau
    )
    weight = jnp.exp(similarity_grid - query_lse[:, None]) + jnp.exp(
        similarity_grid - key_lse[None, :]
    )
    if self_mask is not None:
        weight = jnp.where(self_mask, 0.0, weight)
    return jnp.dot(
        weight.astype(jnp.bfloat16), candidate_embeddings, preferred_element_type=jnp.float32
    )


def body(embed, partner, plan):
    rows = embed.shape[0]
    inverse = lax.rsqrt(jnp.sum(embed * embed, axis=1, keepdims=True) + 1e-06)
    unit = embed * inverse
    rounded_values = unit.astype(jnp.bfloat16)
    own_block = lax.all_gather(rounded_values, "row", axis=0, tiled=True)
    everyone = lax.all_gather(rounded_values, "block", axis=0, tiled=True)
    nblock = lax.axis_size("block")
    here = lax.axis_index("block")
    offset = lax.axis_index("row") * rows
    block_rows = own_block.shape[0]
    width = own_block.shape[1]
    opponents = plan[:, here]
    shards = everyone.reshape(nblock, rows, width)[opponents]
    self_mask = (offset + jnp.arange(rows, dtype=jnp.int32))[:, None] == jnp.arange(
        block_rows, dtype=jnp.int32
    )[None, :]
    own_score, own_exp = exp_rows(rounded_values, own_block)
    contrastive_objective = jnp.sum(jnp.where(self_mask, 0.0, own_exp), axis=1)
    opponent_keys = fetch_partner(shards)
    for turn in range(ROUNDS):
        unused, similarity_exps = exp_rows(rounded_values, opponent_keys[turn])
        contrastive_objective = contrastive_objective + jnp.sum(similarity_exps, axis=1)
    log_partition = inverse_tau + jnp.log(contrastive_objective)
    partner_embedding_block = own_block[partner].astype(jnp.float32)
    matched_similarity = inverse_tau * jnp.sum(
        rounded_values.astype(jnp.float32) * partner_embedding_block, axis=1
    )
    loss = lax.psum(jnp.sum(log_partition - matched_similarity), ("block", "row")) / (
        nblock * block_rows
    )
    block_values = lax.all_gather(log_partition, "row", axis=0, tiled=True)
    every_value = lax.all_gather(block_values, "block", axis=0, tiled=True).reshape(
        nblock, block_rows
    )
    opponent_lse = every_value[opponents]
    exp_accumulator = weighted_keys(
        rounded_values, own_block, log_partition, block_values, self_mask
    )
    for turn in range(ROUNDS):
        exp_accumulator = exp_accumulator + weighted_keys(
            rounded_values, opponent_keys[turn], log_partition, opponent_lse[turn], None
        )
    normalized_embedding = inverse_tau * (exp_accumulator - 2.0 * partner_embedding_block)
    grad = inverse * (
        normalized_embedding - unit * jnp.sum(unit * normalized_embedding, axis=1, keepdims=True)
    )
    return (grad, log_partition, loss)


def solution(mesh):
    placed = (P(("block", "row"), None), P(("block", "row")), P())
    return jax.shard_map(
        body,
        mesh=mesh,
        in_specs=placed,
        out_specs=(P(("block", "row"), None), P(("block", "row")), P()),
        check_vma=False,
    )
```

profile of v0, /device:TPU:1, one launch (start us, length us, event | category | flops | bytes accessed | tf_op | source)
XLA Modules:
  0.0 517.4 jit_solution(16422351016577807836)
XLA Ops:
  7.2 1.1 multiply_reduce_fusion.1
  8.3 1.1 copy.15
  9.4 0.7 multiply_convert_fusion
  10.1 0.7 all-gather.6.cloned.1.call-update
  10.8 0.9 fusion.8
  11.7 71.3 %all-gather.8.cloned.1.call-done = bf16[12288,128]{0,1:T(8,128)(2,1)} async-done(((bf16[384,128]{0,1:T(8,128)(2,1)}), bf16[12288,128]{0,1:T(8,128)(2,1)}) %all-gather.8.cloned.1.call-update) | async-done | bytes 3145744 | tf_op jit(solution)/shard_map/all_gather | solution.py:49
  83.0 3.5 copy.20
  86.5 1.2 gather_fusion
  87.8 0.7 compare_select_fusion
  88.4 85.5 %all-gather.6.cloned.1.call-done = bf16[6144,128]{0,1:T(8,128)(2,1)} async-done(((bf16[384,128]{0,1:T(8,128)(2,1)}), bf16[6144,128]{0,1:T(8,128)(2,1)}) %all-gather.6.cloned.1.call-update) | async-done | bytes 1572880 | tf_op jit(solution)/shard_map/all_gather | solution.py:48
  174.0 1.9 copy.17
  175.9 1.4 gather_fusion.2
  177.5 8.0 %select_reduce_fusion = (f32[384]{0:T(512)S(1)}, f32[384,6144]{1,0:T(8,128)}) fusion(s32[384]{0:T(512)S(1)} %iota_add_fusion, bf16[384,128]{0,1:T(8,128)(2,1)S(1)} %copy-done, bf16[6144,128]{0,1:T(8,128)(2,1)} %all-gather.6.cloned.1.call-done), kind=kOutput, calls=%fused_computation.8 | convolution fusion | flops 615775872 | bytes 11111424 | tf_op jit(solution)/shard_map/qe,ke->qk/dot_general | solution.py:28
  185.5 101.0 %all-gather.10.cloned.1.call-done = bf16[2,6144,128]{2,1,0:T(8,128)(2,1)} async-done(((bf16[2,384,128]{2,1,0:T(8,128)(2,1)}), bf16[2,6144,128]{2,1,0:T(8,128)(2,1)}) %all-gather.10.cloned.1.call-update) | async-done | bytes 3145744 | tf_op jit(solution)/shard_map/all_gather | solution.py:13
  286.6 7.2 %exponential_reduce_fusion.1 = (f32[384]{0:T(512)S(1)}, f32[384,6144]{1,0:T(8,128)}) fusion(bf16[384,128]{0,1:T(8,128)(2,1)S(1)} %copy-done, bf16[2,6144,128]{2,1,0:T(8,128)(2,1)} %all-gather.10.cloned.1.call-done), kind=kOutput, calls=%fused_computation.7 | convolution fusion | flops 611057280 | bytes 11109888 | tf_op jit(solution)/shard_map/qe,ke->qk/dot_general | solution.py:18
  293.7 4.7 exponential_reduce_fusion
  298.4 0.6 subtract_reduce_fusion
  299.1 102.5 %psum.7 = f32[]{:T(128)} all-reduce(f32[]{:T(128)} %get-tuple-element.12), channel_id=1, replica_groups=mesh['block'=32,'row'=16] {'block','row'}, use_global_device_ids=true, to_apply=%region_7.8 | all-reduce | flops 1 | bytes 8 | tf_op jit(solution)/shard_map/psum | solution.py:71
  401.6 41.6 %all-gather.1 = f32[16,1,384]{2,1,0:T(1,128)S(1)} all-gather(f32[1,1,384]{2,1,0:T(1,128)S(1)} %reshape.62), channel_id=1, replica_groups=mesh['block'=32,'row'=16] {'row'}, dimensions={0}, use_global_device_ids=true | all-gather | bytes 26112 | tf_op jit(solution)/shard_map/all_gather | solution.py:74
  443.2 50.2 %all_gather.19 = f32[196608]{0:T(1024)S(1)} all-gather(f32[6144]{0:T(1024)S(1)} %bitcast.24), channel_id=1, replica_groups=mesh['block'=32,'row'=16] {'block'}, dimensions={0}, use_global_device_ids=true | all-gather | bytes 811008 | tf_op jit(solution)/shard_map/all_gather | solution.py:75
  494.2 7.0 %fusion = f32[384,128]{0,1:T(8,128)S(1)} fusion(f32[384,6144]{1,0:T(8,128)} %get-tuple-element.21, f32[6144]{0:T(1024)S(1)} %bitcast.27, f32[384]{0:T(512)S(1)} %get-tuple-element.13, bf16[2,6144,128]{2,1,0:T(8,128)(2,1)} %all-gather.10.cloned.1.call-done), kind=kOutput, calls=%fused_computation.13 | convolution fusion | flops 613416960 | bytes 11232768 | tf_op jit(solution)/shard_map/dot_general | solution.py:38
  501.7 2.8 fusion.1
  504.9 3.4 multiply_reduce_fusion
  508.3 0.8 copy.19
  (40 shorter events, 1.9 us)
Async XLA Ops:
  7.2 75.8 %all-gather.8.cloned.1.call-start = ((), (), s32[]{:S(2)}) async-start(), calls=%async_computation.1 | async-start | bytes 3244032 | tf_op jit(solution)/shard_map/all_gather | solution.py:49
  10.0 167.5 %copy-start = (bf16[384,128]{0,1:T(8,128)(2,1)S(1)}, bf16[384,128]{0,1:T(8,128)(2,1)}, u32[]{:S(2)}) copy-start(bf16[384,128]{0,1:T(8,128)(2,1)} %multiply_convert_fusion) | copy-start | bytes 294916
  10.0 163.9 %all-gather.6.cloned.1.call-start = ((), (), s32[]{:S(2)}) async-start(), calls=%async_computation | async-start | bytes 1671168 | tf_op jit(solution)/shard_map/all_gather | solution.py:48
  10.8 275.8 %all-gather.10.cloned.1.call-start = ((), (), s32[]{:S(2)}) async-start(), calls=%async_computation.2 | async-start | bytes 3342336 | tf_op jit(solution)/shard_map/all_gather | solution.py:13
  286.6 7.2 %copy-start.1 = (bf16[2,6144,128]{2,1,0:T(8,128)(2,1)S(1)}, bf16[2,6144,128]{2,1,0:T(8,128)(2,1)}, u32[]{:S(2)}) copy-start(bf16[2,6144,128]{2,1,0:T(8,128)(2,1)} %all-gather.10.cloned.1.call-done) | copy-start | bytes 9437188
  299.1 205.4 %copy-start.4 = (f32[384]{0:T(512)}, f32[384]{0:T(512)S(1)}, u32[]{:S(2)}) copy-start(f32[384]{0:T(512)S(1)} %get-tuple-element.13) | copy-start | bytes 4612
  493.5 7.7 %slice-start = ((s8[9437184]{0:T(1024)(128)(4,1)}), s8[1048576]{0:T(1024)(128)(4,1)S(1)}, s32[]{:S(2)}) async-start(s8[9437184]{0:T(1024)(128)(4,1)} %bitcast.21), calls=%async_computation.3 | async-start | bytes 2097152
  494.1 7.2 %copy-start.2 = (bf16[2,6144,128]{2,1,0:T(8,128)(2,1)S(1)}, bf16[2,6144,128]{2,1,0:T(8,128)(2,1)}, u32[]{:S(2)}) copy-start(bf16[2,6144,128]{2,1,0:T(8,128)(2,1)} %all-gather.10.cloned.1.call-done) | copy-start | bytes 9437188
  494.2 7.1 %slice-start.1 = ((s8[9437184]{0:T(1024)(128)(4,1)}), s8[4194304]{0:T(1024)(128)(4,1)S(1)}, s32[]{:S(2)}) async-start(s8[9437184]{0:T(1024)(128)(4,1)} %bitcast.21), calls=%async_computation.4 | async-start | bytes 8388608
  494.2 7.5 %slice-start.2 = ((s8[9437184]{0:T(1024)(128)(4,1)}), s8[4194304]{0:T(1024)(128)(4,1)S(1)}, s32[]{:S(2)}) async-start(s8[9437184]{0:T(1024)(128)(4,1)} %bitcast.21), calls=%async_computation.5 | async-start | bytes 8388608
  494.2 10.3 %slice-start.3 = ((s8[9437184]{0:T(1024)(128)(4,1)}), s8[4194304]{0:T(1024)(128)(4,1)S(1)}, s32[]{:S(2)}) async-start(s8[9437184]{0:T(1024)(128)(4,1)} %bitcast.28), calls=%async_computation.6 | async-start | bytes 8388608
  494.2 10.3 %slice-start.4 = ((s8[9437184]{0:T(1024)(128)(4,1)}), s8[4194304]{0:T(1024)(128)(4,1)S(1)}, s32[]{:S(2)}) async-start(s8[9437184]{0:T(1024)(128)(4,1)} %bitcast.28), calls=%async_computation.7 | async-start | bytes 8388608
  501.2 3.4 copy-start.3
  501.7 3.2 slice-start.5
Sparse Core Ops, SparseCore 0:
  10.2 72.7 all-gather.7
  86.0 87.9 all-gather.5
  177.5 108.9 all-gather.9
where the time goes:
time: 518 us; the launch traced here: 517 us
  waiting for transfers between devices  259 us (50%)
  blocking collectives  194 us (37%)
  matrix products  33.2 us (6%)
  between operations  15.7 us (3%)
  local copies, waits for them, and re-layouts  11.6 us (2%)
    psum x1, blocking collectives, body(): lax.psum(jnp.sum(log_partition - matched_similarity), ('block', 'row'))  103 us
    all_gather x1, waiting for transfers between devices, fetch_partner(): return lax.all_gather(shards, 'row', axis=1, tiled=True)  101 us
    all_gather x1, waiting for transfers between devices, body(): own_block = lax.all_gather(rounded_values, 'row', axis=0, tiled=True)  85.5 us
    all_gather x1, waiting for transfers between devices, body(): everyone = lax.all_gather(rounded_values, 'block', axis=0, tiled=True)  71.3 us
    all_gather x1, blocking collectives, body(): lax.all_gather(block_values, 'block', axis=0, tiled=True)  50.2 us
    all_gather x1, blocking collectives, body(): block_values = lax.all_gather(log_partition, 'row', axis=0, tiled=True)  41.6 us
    dot_general x3, matrix products, weighted_keys(): jnp.dot(weight.astype(jnp.bfloat16), candidate_embeddings, preferred_elem...  13.3 us
    dot_general x2, matrix products, exp_rows(): jnp.einsum('qe,ke->qk', anchor_embeddings, candidate_embeddings, preferre...  11.9 us
  transfers between devices with their start and end apart: 3, of which 3 were waited for; matrix products, arithmetic and copies ran while one was open for 3% of the time, Pallas kernels for 0%

commit v1 on v0

v1 whole, which is shorter than its diff:
```python
import functools

import jax
import jax.numpy as jnp
import numpy as np
from jax import lax
from jax.experimental import pallas as pl
from jax.experimental.pallas import tpu as pltpu
from jax.sharding import Mesh
from jax.sharding import PartitionSpec as P

ROUNDS = 2
INVERSE_TAU = 10.0
LOG2E = float(np.log2(np.e))
SCALE = INVERSE_TAU * LOG2E

AXES = ("zl", "y", "c", "x", "zh")
SIZES = (4, 4, 2, 4, 4)
BLOCK = ("zl", "y", "c")
COLUMN = ("zh", "zl")
PLANE = ("y", "c", "x")

R = 384
E = 128
N_BLOCK = 32
N_X = 4
N_ZH = 4
N_ZL = 4
BLOCK_ROWS = R * N_X * N_ZH
CHUNK = 16
KEYS = 3 * R
PACK = KEYS + 16
OUT = R + 16
VMEM = 56 * 1024 * 1024

whole = pl.BlockSpec(memory_space=pltpu.VMEM)
smem = pl.BlockSpec(memory_space=pltpu.SMEM)


def to_column(row):
    return jnp.transpose(jnp.broadcast_to(row, (E, R)))


def lanes(wide):
    return jnp.concatenate([wide] * (R // E), axis=1)


def partner_row(keys_ref, xp):
    parts = keys_ref[xp, KEYS:PACK, :].astype(jnp.float32)
    pieces = [parts[i : i + 1] * 128.0 + parts[3 + i : 4 + i] for i in range(3)]
    return jnp.concatenate(pieces, axis=1).astype(jnp.int32)


def select_kernel(plan_ref, chunks_ref, out_ref):
    for b in range(N_BLOCK):
        for t in range(ROUNDS):
            out_ref[b, t] = chunks_ref[plan_ref[t, b]]


def pack_kernel(rounded_ref, opponents_ref, partner_ref, out_ref):
    index = partner_ref[...]
    high = index // 128
    low = index - high * 128
    both = jnp.concatenate([high, low, jnp.zeros((10, E), jnp.int32)], axis=0)
    index = both.astype(jnp.float32).astype(jnp.bfloat16)
    for xp in range(N_X):
        out_ref[xp, 0:R] = rounded_ref[...]
        for t in range(ROUNDS):
            for k in range(R // CHUNK):
                at = (t + 1) * R + k * CHUNK
                out_ref[xp, at : at + CHUNK] = opponents_ref[k, t]
        out_ref[xp, KEYS:PACK] = index


def partition_kernel(queries_ref, keys_ref, exp_ref, sums_ref, positive_ref):
    piece = pl.program_id(0)
    x = lax.axis_index("x")
    zh = lax.axis_index("zh")
    q = queries_ref[(zh - piece + N_ZH) % N_ZH]
    base = x * (R * N_ZH) + piece * R
    row = lax.broadcasted_iota(jnp.int32, (R, R), 0)
    diagonal = row - lax.broadcasted_iota(jnp.int32, (R, R), 1)
    total = jnp.zeros((R, E), jnp.float32)
    positive = jnp.zeros((R, E), jnp.float32)
    for xp in range(N_X):
        for t in range(ROUNDS + 1):
            k = keys_ref[xp, t * R : (t + 1) * R, :]
            s = lax.dot_general(q, k, (((1,), (1,)), ((), ())), preferred_element_type=jnp.float32)
            e = jnp.exp2(s * SCALE - SCALE)
            if t == 0:
                e = jnp.where(diagonal == xp * (R * N_ZH) + zh * R - base, 0.0, e)
                mine = jnp.where(row == partner_row(keys_ref, xp) - base, s, 0.0)
                for i in range(R // E):
                    positive = positive + mine[:, i * E : (i + 1) * E]
            for i in range(R // E):
                total = total + e[:, i * E : (i + 1) * E]
            at = (xp * 3 + t) * R
            exp_ref[:, at : at + R] = e.astype(jnp.bfloat16)
    sums_ref[0] = lax.dot_general(
        jnp.ones((8, E), jnp.float32), total, (((1,), (1,)), ((), ())),
        precision=lax.Precision.HIGHEST, preferred_element_type=jnp.float32,
    )

    @pl.when(piece == 0)
    def _():
        positive_ref[...] = jnp.zeros_like(positive_ref)

    positive_ref[...] += jnp.sum(positive.reshape(R // 8, 8, E), axis=0)


def direction_kernel(plan_ref, exp_ref, queries_ref, keys_ref, own_ref, sums_ref, out_ref):
    piece = pl.program_id(0)
    zl, y, c = (lax.axis_index(a) for a in BLOCK)
    x = lax.axis_index("x")
    zh = lax.axis_index("zh")
    here = (zl * 4 + y) * 2 + c
    q = queries_ref[(zh - piece + N_ZH) % N_ZH]
    base = x * (R * N_ZH) + piece * R
    row = lax.broadcasted_iota(jnp.int32, (R, R), 0)
    column = lanes(to_column(1.0 / own_ref[pl.ds(piece, 1), :]))
    total = jnp.zeros((R, E), jnp.float32)
    for t in range(ROUNDS + 1):
        other = here if t == 0 else plan_ref[t - 1, here]
        level = other // 8
        place = other - level * 8
        for xp in range(N_X):
            k = keys_ref[xp, t * R : (t + 1) * R, :]
            at = (xp * 3 + t) * R
            inverse = 1.0 / sums_ref[pl.ds(place * N_X + xp, 1), pl.ds(pl.multiple_of(level * R, 128), R)]
            w = exp_ref[:, at : at + R].astype(jnp.float32) * (column + inverse)
            if t == 0:
                w = w - jnp.where(row == partner_row(keys_ref, xp) - base, 2.0, 0.0)
            total = total + jnp.dot(w.astype(jnp.bfloat16), k, preferred_element_type=jnp.float32)
    wide = q.astype(jnp.float32)
    along = jnp.sum(total * wide, axis=1, keepdims=True).astype(jnp.bfloat16).astype(jnp.float32)
    out_ref[0, 0:R] = (total - along * wide).astype(jnp.bfloat16)
    first = lax.broadcasted_iota(jnp.int32, (R, E), 1) == 0
    line = lax.dot_general(
        jnp.ones((8, E), jnp.bfloat16), jnp.where(first, along, 0.0).astype(jnp.bfloat16),
        (((1,), (1,)), ((), ())), preferred_element_type=jnp.float32,
    )
    line = [line[0:1, i * E : (i + 1) * E] for i in range(R // E)]
    line = jnp.concatenate(line + [jnp.zeros((16 - R // E, E), jnp.float32)], axis=0)
    out_ref[0, R:OUT] = line.astype(jnp.bfloat16)


def finish_kernel(embed_ref, parts_ref, out_ref):
    x = embed_ref[...]
    inverse = lax.rsqrt(jnp.sum(x * x, axis=1, keepdims=True) + 1e-06)
    unit = x * inverse
    rounded = unit.astype(jnp.bfloat16).astype(jnp.float32)
    total = jnp.zeros((R, E), jnp.float32)
    line = jnp.zeros((16, E), jnp.float32)
    for z in range(N_ZH):
        total = total + parts_ref[z, 0:R].astype(jnp.float32)
        line = line + parts_ref[z, R:OUT].astype(jnp.float32)
    along = to_column(jnp.concatenate([line[i : i + 1] for i in range(R // E)], axis=1))
    direction = INVERSE_TAU * (total + along * rounded)
    out_ref[...] = inverse * (direction - unit * jnp.sum(unit * direction, axis=1, keepdims=True))


def params(**more):
    return pltpu.CompilerParams(vmem_limit_bytes=VMEM, **more)


def f32(*shape):
    return jax.ShapeDtypeStruct(shape, jnp.float32)


def bf16(*shape):
    return jax.ShapeDtypeStruct(shape, jnp.bfloat16)


def exchange(value, axes):
    return lax.all_to_all(value, axes, 0, 0, tiled=True)


def body(embed, partner, plan):
    zl = lax.axis_index("zl")
    zh = lax.axis_index("zh")
    with jax.named_scope("normalize"):
        inverse = lax.rsqrt(jnp.sum(embed * embed, axis=1, keepdims=True) + 1e-06)
        rounded = (embed * inverse).astype(jnp.bfloat16)
    with jax.named_scope("queries"):
        queries = [rounded]
        for shift in (1, 2, 3):
            queries.append(lax.ppermute(rounded, "zh", [(i, (i + shift) % N_ZH) for i in range(N_ZH)]))
        queries = jnp.stack(queries)
    with jax.named_scope("opponents"):
        padded = jnp.concatenate([rounded, rounded[: N_BLOCK * CHUNK - R]])
        chunks = exchange(padded.reshape(N_BLOCK, CHUNK, E), BLOCK)
        chosen = pl.pallas_call(
            select_kernel, out_shape=bf16(N_BLOCK, ROUNDS, CHUNK, E), in_specs=[smem, whole], out_specs=whole,
            compiler_params=params(),
        )(plan, chunks)
        chosen = exchange(chosen, BLOCK)
    with jax.named_scope("keys"):
        packed = pl.pallas_call(
            pack_kernel, out_shape=bf16(N_X, PACK, E), in_specs=[whole] * 3, out_specs=whole,
            compiler_params=params(),
        )(rounded, chosen, partner.reshape(3, 128))
        keys = exchange(packed, "x")
    with jax.named_scope("partition"):
        exps, sums, positive = pl.pallas_call(
            partition_kernel,
            grid=(N_ZH,),
            out_shape=(bf16(N_ZH * R, N_X * KEYS), f32(N_ZH, 8, R), f32(8, E)),
            in_specs=[whole, whole],
            out_specs=(
                pl.BlockSpec((R, N_X * KEYS), lambda g: (g, 0)),
                pl.BlockSpec((1, 8, R), lambda g: (g, 0, 0)),
                pl.BlockSpec((8, E), lambda g: (0, 0)),
            ),
            compiler_params=params(),
        )(queries, keys)
    with jax.named_scope("sums"):
        line = jnp.concatenate([sums[:, 0, :].reshape(N_ZH * R), jnp.full((E,), jnp.sum(positive))])
        line = exchange(jnp.broadcast_to(line, (N_ZH * N_ZL, N_ZH * R + E)), COLUMN)
        line = jnp.sum(line.reshape(N_ZH, N_ZL, N_ZH * R + E), axis=0)
        parts = line[:, : N_ZH * R].reshape(N_ZL, N_ZH, R)
        mine = lax.dynamic_index_in_dim(parts, zl, 0, keepdims=False)
        log_partition = INVERSE_TAU + jnp.log(lax.dynamic_index_in_dim(mine, zh, 0, keepdims=False))
        column_loss = jnp.sum(INVERSE_TAU + jnp.log(parts)) - INVERSE_TAU * jnp.sum(line[:, N_ZH * R])
        level = lax.dynamic_index_in_dim(parts, zh, 1, keepdims=False).reshape(N_ZL * R)
        level = jnp.concatenate([level, jnp.full((E,), column_loss)])
        level = exchange(jnp.broadcast_to(level, (32, N_ZL * R + E)), PLANE)
        loss = jnp.sum(level[:, N_ZL * R]) / (N_BLOCK * BLOCK_ROWS)
    with jax.named_scope("direction"):
        out = pl.pallas_call(
            direction_kernel,
            grid=(N_ZH,),
            out_shape=bf16(N_ZH, OUT, E),
            in_specs=[smem, pl.BlockSpec((R, N_X * KEYS), lambda g: (g, 0)), whole, whole, whole, whole],
            out_specs=pl.BlockSpec((1, OUT, E), lambda g: (g, 0, 0)),
            compiler_params=params(),
        )(plan, exps, queries, keys, mine, level)
        out = exchange(out, "zh")
    with jax.named_scope("finish"):
        grad = pl.pallas_call(
            finish_kernel, out_shape=f32(R, E), in_specs=[whole] * 2, out_specs=whole, compiler_params=params(),
        )(embed, out)
    return (grad, log_partition, loss)


def solution(mesh):
    split = Mesh(mesh.devices.reshape(SIZES), AXES)
    return jax.shard_map(
        body,
        mesh=split,
        in_specs=(P(AXES, None), P(AXES), P()),
        out_specs=(P(AXES, None), P(AXES), P()),
        check_vma=False,
    )
```

time: 518 us -> 184 us (0.36)
  the two profiles are of different devices: /device:TPU:1 before, /device:TPU:32 now
where the time goes in v1:
time: 184 us; the launch traced here: 183 us
  waiting for transfers between devices  57.4 us (31%)
  starting transfers between devices  46 us (25%)
  blocking collectives  32.2 us (18%)
  Pallas kernels  29.2 us (16%)
  other arithmetic  7.78 us (4%)
  local copies, waits for them, and re-layouts  6.18 us (3%)
  between operations  3.86 us (2%)
    all_to_all x4, waiting for transfers between devices, exchange(): return lax.all_to_all(value, axes, 0, 0, tiled=True)  45.7 us
    all_to_all x2, blocking collectives, exchange(): return lax.all_to_all(value, axes, 0, 0, tiled=True)  32.2 us
    all_to_all x4, starting transfers between devices, exchange(): return lax.all_to_all(value, axes, 0, 0, tiled=True)  23.2 us
    ppermute x3, starting transfers between devices, body(): lax.ppermute(rounded, 'zh', [(i, (i + shift) % N_ZH) for i in range(N_ZH)])  22.8 us
    pallas_call x1, Pallas kernels, body(): pl.pallas_call(partition_kernel, grid=(N_ZH,), out_shape=(bf16(N_ZH * R,...  13.1 us
    ppermute x3, waiting for transfers between devices, body(): lax.ppermute(rounded, 'zh', [(i, (i + shift) % N_ZH) for i in range(N_ZH)])  11.7 us
    pallas_call x1, Pallas kernels, body(): pl.pallas_call(direction_kernel, grid=(N_ZH,), out_shape=bf16(N_ZH, OUT,...  10.2 us
  transfers between devices with their start and end apart: 7, of which 5 were waited for; matrix products, arithmetic and copies ran while one was open for 2% of the time, Pallas kernels for 0%

profile of v1, /device:TPU:32, one launch (start us, length us, event | category | flops | bytes accessed | tf_op | source)
XLA Modules:
  0.0 182.6 jit_solution(13169444043986820932)
XLA Ops:
  0.6 1.1 multiply_reduce_fusion
  1.7 1.0 multiply_convert_fusion.rounded_ref
  2.8 16.3 %all_to_all.34.chunks_ref = bf16[32,16,128]{2,1,0:T(8,128)(2,1)} all-to-all(bf16[32,16,128]{2,1,0:T(8,128)(2,1)S(1)} %bitcast.14), channel_id=1, replica_groups=mesh['zl'=4,'y'=4,'c'=2,'x'=4,'zh'=4] {'zl','y','c'}, dimensions={0} | all-to-all | bytes 262144 | tf_op jit(solution)/shard_map/opponents/all_to_all | solution.py:175
  19.1 1.7 opponents.1
  20.8 15.9 %all_to_all.35.opponents_ref = bf16[32,2,16,128]{3,2,1,0:T(8,128)(2,1)} all-to-all(bf16[32,2,16,128]{3,2,1,0:T(8,128)(2,1)} %opponents.1), channel_id=1, replica_groups=mesh['zl'=4,'y'=4,'c'=2,'x'=4,'zh'=4] {'zl','y','c'}, dimensions={0} | all-to-all | bytes 524288 | tf_op jit(solution)/shard_map/opponents/all_to_all | solution.py:175
  36.7 2.1 %keys.1 = bf16[4,1168,128]{2,1,0:T(8,128)(2,1)} custom-call(bf16[384,128]{1,0:T(8,128)(2,1)} %copy-done.3, bf16[32,2,16,128]{3,2,1,0:T(8,128)(2,1)} %all_to_all.35.opponents_ref, s32[3,128]{1,0:T(4,128)} %bitcast.18), custom_call_target="tpu_custom_call" | custom-call | tf_op jit(solution)/shard_map/keys/pallas_call | solution.py:198
  38.8 4.2 %all-to-all-start.2 = ((bf16[4,1168,128]{2,1,0:T(8,128)(2,1)}), bf16[4,1168,128]{2,1,0:T(8,128)(2,1)S(1)}, u32[]{:S(2)}, u32[]{:S(2)}) async-start(bf16[4,1168,128]{2,1,0:T(8,128)(2,1)} %keys.1), calls=%async_computation.2 | async-start | bytes 2392064 | tf_op jit(solution)/shard_map/keys/all_to_all | solution.py:175
  43.0 10.0 %collective-permute-start.2 = (bf16[384,128]{1,0:T(8,128)(2,1)S(1)}, bf16[384,128]{1,0:T(8,128)(2,1)S(1)}, u32[]{:S(2)}, u32[]{:S(2)}) collective-permute-start(bf16[384,128]{1,0:T(8,128)(2,1)S(1)} %copy-done.4), channel_id=1, source_target_pairs={{0,3},{1,0},{2,1},{3,2},{4,7},{5,4},{6,5},{7,6},{8,11},{9,8},{10,9... | collective-permute-start | bytes 294920 | tf_op jit(solution)/shard_map/queries/ppermute | solution.py:187
  53.1 6.3 %collective-permute-start.1 = (bf16[384,128]{1,0:T(8,128)(2,1)S(1)}, bf16[384,128]{1,0:T(8,128)(2,1)S(1)}, u32[]{:S(2)}, u32[]{:S(2)}) collective-permute-start(bf16[384,128]{1,0:T(8,128)(2,1)S(1)} %copy-done.4), channel_id=1, source_target_pairs={{0,2},{1,3},{2,0},{3,1},{4,6},{5,7},{6,4},{7,5},{8,10},{9,11},{10,... | collective-permute-start | bytes 294920 | tf_op jit(solution)/shard_map/queries/ppermute | solution.py:187
  59.4 6.4 %collective-permute-start = (bf16[384,128]{1,0:T(8,128)(2,1)S(1)}, bf16[384,128]{1,0:T(8,128)(2,1)S(1)}, u32[]{:S(2)}, u32[]{:S(2)}) collective-permute-start(bf16[384,128]{1,0:T(8,128)(2,1)S(1)} %copy-done.4), channel_id=1, source_target_pairs={{0,1},{1,2},{2,3},{3,0},{4,5},{5,6},{6,7},{7,4},{8,9},{9,10},{10,1... | collective-permute-start | bytes 294920 | tf_op jit(solution)/shard_map/queries/ppermute | solution.py:187
  66.0 2.4 %collective-permute-done.1 = bf16[384,128]{1,0:T(8,128)(2,1)S(1)} collective-permute-done((bf16[384,128]{1,0:T(8,128)(2,1)S(1)}, bf16[384,128]{1,0:T(8,128)(2,1)S(1)}, u32[]{:S(2)}, u32[]{:S(2)}) %collective-permute-start.1) | collective-permute-done | bytes 98336 | tf_op jit(solution)/shard_map/queries/ppermute | solution.py:187
  68.4 9.3 %collective-permute-done = bf16[384,128]{1,0:T(8,128)(2,1)S(1)} collective-permute-done((bf16[384,128]{1,0:T(8,128)(2,1)S(1)}, bf16[384,128]{1,0:T(8,128)(2,1)S(1)}, u32[]{:S(2)}, u32[]{:S(2)}) %collective-permute-start) | collective-permute-done | bytes 98336 | tf_op jit(solution)/shard_map/queries/ppermute | solution.py:187
  78.5 1.0 copy-done
  79.6 13.1 %partition.1 = (bf16[1536,4608]{1,0:T(8,128)(2,1)}, f32[4,8,384]{2,1,0:T(8,128)}, f32[8,128]{1,0:T(8,128)}) custom-call(bf16[4,384,128]{2,1,0:T(8,128)(2,1)} %pad_maximum_fusion.queries_ref, bf16[4,1168,128]{2,1,0:T(8,128)(2,1)} %copy-done), custom_call_target="tpu_custom_call" | custom-call | tf_op jit(solution)/shard_map/partition/pallas_call | solution.py:204
  93.5 1.3 reduce_sum.55
  96.1 10.0 %all-to-all-start.3 = ((f32[16,1,1664]{2,1,0:T(1,128)}), f32[16,1,1664]{2,1,0:T(1,128)S(1)}, u32[]{:S(2)}, u32[]{:S(2)}) async-start(f32[16,1,1664]{2,1,0:T(1,128)} %broadcast_in_dim.4), calls=%async_computation.3 | async-start | bytes 212992 | tf_op jit(solution)/shard_map/sums/all_to_all | solution.py:175
  106.1 13.4 %all-to-all-done.3 = f32[16,1,1664]{2,1,0:T(1,128)S(1)} async-done(((f32[16,1,1664]{2,1,0:T(1,128)}), f32[16,1,1664]{2,1,0:T(1,128)S(1)}, u32[]{:S(2)}, u32[]{:S(2)}) %all-to-all-start.3) | async-done | bytes 106528 | tf_op jit(solution)/shard_map/sums/all_to_all | solution.py:175
  123.3 5.5 %all-to-all-start.4 = ((f32[32,1,1664]{2,1,0:T(1,128)}), f32[32,1,1664]{2,1,0:T(1,128)S(1)}, u32[]{:S(2)}, u32[]{:S(2)}) async-start(f32[32,1,1664]{2,1,0:T(1,128)} %broadcast_in_dim.10), calls=%async_computation.4 | async-start | bytes 425984 | tf_op jit(solution)/shard_map/sums/all_to_all | solution.py:175
  129.3 7.7 %all-to-all-done.4 = f32[32,1,1664]{2,1,0:T(1,128)S(1)} async-done(((f32[32,1,1664]{2,1,0:T(1,128)}), f32[32,1,1664]{2,1,0:T(1,128)S(1)}, u32[]{:S(2)}, u32[]{:S(2)}) %all-to-all-start.4) | async-done | bytes 213024 | tf_op jit(solution)/shard_map/sums/all_to_all | solution.py:175
  137.7 10.2 %direction.1 = bf16[4,400,128]{2,1,0:T(8,128)(2,1)} custom-call(s32[2,32]{1,0:T(2,128)} %plan_ref.3, bf16[1536,4608]{1,0:T(8,128)(2,1)} %get-tuple-element.6.exp_ref, bf16[4,384,128]{2,1,0:T(8,128)(2,1)} %pad_maximum_fusion.queries_ref, bf16[4,1168,128]{2,1,0:T(8,128)(2,1)} %copy-done, f32[4,384]{1,0:T(4,128)} %dynamic-slice_bitcast_fusion.own_ref, ...), custom_call_target="tpu_custom_call" | custom-call | tf_op jit(solution)/shard_map/direction/pallas_call | solution.py:229
  148.0 3.5 %all-to-all-start.5 = ((bf16[4,400,128]{2,1,0:T(8,128)(2,1)}), bf16[4,400,128]{2,1,0:T(8,128)(2,1)S(1)}, u32[]{:S(2)}, u32[]{:S(2)}) async-start(bf16[4,400,128]{2,1,0:T(8,128)(2,1)} %direction.1), calls=%async_computation.5 | async-start | bytes 819200 | tf_op jit(solution)/shard_map/direction/all_to_all | solution.py:175
  152.1 1.3 slice_reduce_fusion
  154.1 24.6 %all-to-all-done.5.parts_ref = bf16[4,400,128]{2,1,0:T(8,128)(2,1)S(1)} async-done(((bf16[4,400,128]{2,1,0:T(8,128)(2,1)}), bf16[4,400,128]{2,1,0:T(8,128)(2,1)S(1)}, u32[]{:S(2)}, u32[]{:S(2)}) %all-to-all-start.5) | async-done | bytes 409632 | tf_op jit(solution)/shard_map/direction/all_to_all | solution.py:175
  179.4 2.1 %finish.1 = f32[384,128]{1,0:T(8,128)} custom-call(f32[384,128]{1,0:T(8,128)} %embed_ref.1, bf16[4,400,128]{2,1,0:T(8,128)(2,1)} %copy-done.2), custom_call_target="tpu_custom_call" | custom-call | tf_op jit(solution)/shard_map/finish/pallas_call | solution.py:239
  (33 shorter events, 8.2 us)
Async XLA Ops:
  2.8 33.9 %copy-start.3 = (bf16[384,128]{1,0:T(8,128)(2,1)}, bf16[384,128]{1,0:T(8,128)(2,1)S(1)}, u32[]{:S(2)}) copy-start(bf16[384,128]{1,0:T(8,128)(2,1)S(1)} %multiply_convert_fusion.rounded_ref) | copy-start | bytes 294916
  38.8 4.2 %copy-start.4 = (bf16[384,128]{1,0:T(8,128)(2,1)S(1)}, bf16[384,128]{1,0:T(8,128)(2,1)}, u32[]{:S(2)}) copy-start(bf16[384,128]{1,0:T(8,128)(2,1)} %copy-done.3) | copy-start | bytes 294916
  38.8 27.0 %copy-start.1 = (f32[384,128]{1,0:T(8,128)S(1)}, f32[384,128]{1,0:T(8,128)}, u32[]{:S(2)}) copy-start(f32[384,128]{1,0:T(8,128)} %embed_ref.1) | copy-start | bytes 589828
  38.8 39.7 %all-to-all-start.2 = ((bf16[4,1168,128]{2,1,0:T(8,128)(2,1)}), bf16[4,1168,128]{2,1,0:T(8,128)(2,1)S(1)}, u32[]{:S(2)}, u32[]{:S(2)}) async-start(bf16[4,1168,128]{2,1,0:T(8,128)(2,1)} %keys.1), calls=%async_computation.2 | async-start | bytes 2392064 | tf_op jit(solution)/shard_map/keys/all_to_all | solution.py:175
  43.0 22.9 %collective-permute-start.2 = (bf16[384,128]{1,0:T(8,128)(2,1)S(1)}, bf16[384,128]{1,0:T(8,128)(2,1)S(1)}, u32[]{:S(2)}, u32[]{:S(2)}) collective-permute-start(bf16[384,128]{1,0:T(8,128)(2,1)S(1)} %copy-done.4), channel_id=1, source_target_pairs={{0,3},{1,0},{2,1},{3,2},{4,7},{5,4},{6,5},{7,6},{8,11},{9,8},{10,9... | collective-permute-start | bytes 294920 | tf_op jit(solution)/shard_map/queries/ppermute | solution.py:187
  53.1 15.3 %collective-permute-start.1 = (bf16[384,128]{1,0:T(8,128)(2,1)S(1)}, bf16[384,128]{1,0:T(8,128)(2,1)S(1)}, u32[]{:S(2)}, u32[]{:S(2)}) collective-permute-start(bf16[384,128]{1,0:T(8,128)(2,1)S(1)} %copy-done.4), channel_id=1, source_target_pairs={{0,2},{1,3},{2,0},{3,1},{4,6},{5,7},{6,4},{7,5},{8,10},{9,11},{10,... | collective-permute-start | bytes 294920 | tf_op jit(solution)/shard_map/queries/ppermute | solution.py:187
  59.4 18.3 %collective-permute-start = (bf16[384,128]{1,0:T(8,128)(2,1)S(1)}, bf16[384,128]{1,0:T(8,128)(2,1)S(1)}, u32[]{:S(2)}, u32[]{:S(2)}) collective-permute-start(bf16[384,128]{1,0:T(8,128)(2,1)S(1)} %copy-done.4), channel_id=1, source_target_pairs={{0,1},{1,2},{2,3},{3,0},{4,5},{5,6},{6,7},{7,4},{8,9},{9,10},{10,1... | collective-permute-start | bytes 294920 | tf_op jit(solution)/shard_map/queries/ppermute | solution.py:187
  78.5 1.0 copy-start
  96.1 23.4 %all-to-all-start.3 = ((f32[16,1,1664]{2,1,0:T(1,128)}), f32[16,1,1664]{2,1,0:T(1,128)S(1)}, u32[]{:S(2)}, u32[]{:S(2)}) async-start(f32[16,1,1664]{2,1,0:T(1,128)} %broadcast_in_dim.4), calls=%async_computation.3 | async-start | bytes 212992 | tf_op jit(solution)/shard_map/sums/all_to_all | solution.py:175
  123.3 13.8 %all-to-all-start.4 = ((f32[32,1,1664]{2,1,0:T(1,128)}), f32[32,1,1664]{2,1,0:T(1,128)S(1)}, u32[]{:S(2)}, u32[]{:S(2)}) async-start(f32[32,1,1664]{2,1,0:T(1,128)} %broadcast_in_dim.10), calls=%async_computation.4 | async-start | bytes 425984 | tf_op jit(solution)/shard_map/sums/all_to_all | solution.py:175
  148.0 30.7 %all-to-all-start.5 = ((bf16[4,400,128]{2,1,0:T(8,128)(2,1)}), bf16[4,400,128]{2,1,0:T(8,128)(2,1)S(1)}, u32[]{:S(2)}, u32[]{:S(2)}) async-start(bf16[4,400,128]{2,1,0:T(8,128)(2,1)} %direction.1), calls=%async_computation.5 | async-start | bytes 819200 | tf_op jit(solution)/shard_map/direction/all_to_all | solution.py:175
  178.6 0.7 copy-start.2

commit v2 on v0

v2 whole, which is shorter than its diff:
```python
import jax
import jax.numpy as jnp
import numpy as np
from jax import lax
from jax.experimental import pallas as pl
from jax.experimental.pallas import tpu as pltpu
from jax.sharding import Mesh
from jax.sharding import PartitionSpec as P

ROUNDS = 2
INVERSE_TAU = 10.0
SCALE = INVERSE_TAU * float(np.log2(np.e))

AXES = ("zl", "y", "c", "x", "zh")
SIZES = (4, 4, 2, 4, 4)
BLOCK = ("zl", "y", "c")
PLANE = ("y", "x", "c")
COLUMN = ("zh", "zl")

R = 384
E = 128
N_BLOCK = 32
N_X = 4
N_ZL = 4
N_ZH = 4
GATHERED = R * N_ZH
BLOCK_ROWS = GATHERED * N_X
CHUNK = GATHERED // N_BLOCK
SENT = R + 16
LINES = R // E
SLOT = LINES * N_X
NEAR = 8
LOSS = LINES * NEAR
VMEM = 56 * 1024 * 1024

whole = pl.BlockSpec(memory_space=pltpu.VMEM)
smem = pl.BlockSpec(memory_space=pltpu.SMEM)


def as_row(lines):
    return jnp.concatenate([lines[i : i + 1] for i in range(LINES)], axis=1)


def as_lines(row):
    return jnp.concatenate([row[0:1, i * E : (i + 1) * E] for i in range(LINES)], axis=0)


def to_column(row):
    return jnp.transpose(jnp.broadcast_to(row, (E, R)))


def widen(wide):
    return jnp.concatenate([wide] * LINES, axis=1)


def lane_sums(value):
    return lax.dot_general(
        jnp.ones((8, E), jnp.float32), value, (((1,), (1,)), ((), ())),
        precision=lax.Precision.HIGHEST, preferred_element_type=jnp.float32,
    )


def scores(q, k):
    return lax.dot_general(q, k, (((1,), (1,)), ((), ())), preferred_element_type=jnp.float32)


def normalize_kernel(embed_ref, partner_ref, rounded_ref, sent_ref):
    x = embed_ref[...]
    inverse = lax.rsqrt(jnp.sum(x * x, axis=1, keepdims=True) + 1e-06)
    rounded = (x * inverse).astype(jnp.bfloat16)
    rounded_ref[...] = rounded
    index = partner_ref[...]
    high = index // 128
    low = index - high * 128
    both = jnp.concatenate([high, low, jnp.zeros((16 - 2 * LINES, E), jnp.int32)], axis=0)
    index = both.astype(jnp.float32).astype(jnp.bfloat16)
    for xp in range(N_X):
        sent_ref[xp, 0:R] = rounded
        sent_ref[xp, R:SENT] = index


def select_kernel(plan_ref, chunks_ref, queries_ref, out_ref):
    for b in range(N_BLOCK):
        for t in range(ROUNDS):
            out_ref[b, t] = chunks_ref[plan_ref[t, b]]


def own_kernel(queries_ref, keys_ref, exp_ref, match_ref, sums_ref):
    piece = pl.program_id(0)
    x = lax.axis_index("x")
    zh = lax.axis_index("zh")
    q = queries_ref[0, 0:R]
    index = queries_ref[0, R:SENT].astype(jnp.float32)
    index = as_row(index[0:LINES]) * 128.0 + as_row(index[LINES : 2 * LINES])
    partner = widen(to_column(index)).astype(jnp.int32) - x * GATHERED
    lane = lax.broadcasted_iota(jnp.int32, (R, R), 1)
    itself = lax.broadcasted_iota(jnp.int32, (R, R), 0) + (piece - x) * GATHERED + zh * R
    total = jnp.zeros((R, E), jnp.float32)
    match = jnp.zeros((R, E), jnp.float32)
    for z in range(N_ZH):
        k = keys_ref[z * R : (z + 1) * R]
        e = jnp.exp2(scores(q, k) * SCALE - SCALE)
        e = jnp.where(itself - lane == z * R, 0.0, e)
        for i in range(LINES):
            total = total + e[:, i * E : (i + 1) * E]
        exp_ref[:, z * R : (z + 1) * R] = e.astype(jnp.bfloat16)
        chosen = jnp.where(partner - lane == z * R, 1.0, 0.0).astype(jnp.bfloat16)
        match = match + jnp.dot(chosen, k, preferred_element_type=jnp.float32)
    match_ref[...] = match
    positive = jnp.sum((match * q.astype(jnp.float32)).reshape(R // 8, 8, E), axis=0)
    positive = jnp.broadcast_to(jnp.sum(positive, axis=(0, 1), keepdims=True), (8, R))
    slot = lax.broadcasted_iota(jnp.int32, (8, R), 0)
    sums_ref[0] = jnp.where(slot == 0, lane_sums(total), positive)


def others_kernel(queries_ref, keys_ref, own_ref, exp_ref, line_ref):
    piece = pl.program_id(0)
    q = queries_ref[0, 0:R]
    total = jnp.zeros((R, E), jnp.float32)
    for t in range(ROUNDS):
        for z in range(N_ZH):
            k = jnp.concatenate([keys_ref[z * 8 + i, t] for i in range(8)], axis=0)
            e = jnp.exp2(scores(q, k) * SCALE - SCALE)
            for i in range(LINES):
                total = total + e[:, i * E : (i + 1) * E]
            at = (t * N_ZH + z) * R
            exp_ref[:, at : at + R] = e.astype(jnp.bfloat16)

    @pl.when(piece == 0)
    def _():
        line_ref[...] = jnp.zeros_like(line_ref)

    sums = lane_sums(total)[0:1] + own_ref[0, 0:1]
    sums = as_lines(sums)
    slot = lax.broadcasted_iota(jnp.int32, (16, E), 0)
    line = jnp.where(slot == SLOT, jnp.broadcast_to(own_ref[0, 1:2, 0:E], (16, E)), 0.0)
    for i in range(LINES):
        line = jnp.where(slot == piece * LINES + i, jnp.broadcast_to(sums[i : i + 1], (16, E)), line)
    for i in range(N_BLOCK):
        line_ref[i] += line


def sums_kernel(line_ref, level_ref, mine_ref, log_ref, held):
    near = lax.axis_index("y") * 2 + lax.axis_index("c")
    x = lax.axis_index("x")
    slot = lax.broadcasted_iota(jnp.int32, (16, E), 0)
    loss = jnp.zeros((16, E), jnp.float32)
    for i in range(NEAR):
        y, c = divmod(i, 2)
        part = line_ref[y * 8 + c]
        for j in range(1, N_X):
            part = part + line_ref[y * 8 + j * 2 + c]
        sums = jnp.where(slot < SLOT, part, 1.0)
        logs = INVERSE_TAU + jnp.log(sums)
        loss = loss + jnp.where(slot < SLOT, logs, 0.0)
        loss = loss - jnp.where(slot == SLOT, part * (INVERSE_TAU / E), 0.0)
        held[i, 0] = 1.0 / sums
        held[i, 1] = logs
    mine_ref[...] = held[near, 0]
    log_ref[...] = held[near, 1, pl.ds(x * LINES, LINES), :]
    level = [held[i, 0, pl.ds(x * LINES, LINES), :] for i in range(NEAR)]
    loss = jnp.broadcast_to(jnp.sum(loss, axis=(0, 1), keepdims=True), (1, E))
    for _ in range(3):
        level.append(loss.astype(jnp.bfloat16).astype(jnp.float32))
        loss = loss - level[-1]
    level.append(jnp.zeros((32 - LOSS - 3, E), jnp.float32))
    level = jnp.concatenate(level, axis=0).astype(jnp.bfloat16)
    for i in range(N_ZH * N_ZL):
        level_ref[i] = level


def direction_kernel(plan_ref, own_ref, others_ref, keys_ref, far_ref, match_ref, mine_ref, sums_ref, out_ref, held, both):
    piece = pl.program_id(0)

    @pl.when(piece == 0)
    def _():
        zl, y, c = (lax.axis_index(a) for a in BLOCK)
        here = (zl * 4 + y) * 2 + c
        held[...] = sums_ref[...].astype(jnp.float32)
        for t in range(ROUNDS + 1):
            other = here if t == 0 else plan_ref[t - 1, here]
            level = other // NEAR
            near = other - level * NEAR
            for z in range(N_ZH):
                inverse = to_column(as_row(held[z * N_ZL + level, pl.ds(near * LINES, LINES), :]))
                if t == 0:
                    k = keys_ref[z * R : (z + 1) * R]
                else:
                    k = jnp.concatenate([far_ref[z * 8 + i, t - 1] for i in range(8)], axis=0)
                at = (t * N_ZH + z) * R
                both[at : at + R, 0:E] = k
                both[at : at + R, E : 2 * E] = (k.astype(jnp.float32) * inverse).astype(jnp.bfloat16)

    total = jnp.dot(own_ref[...], both[0:GATHERED], preferred_element_type=jnp.float32)
    total = total + jnp.dot(others_ref[...], both[GATHERED:], preferred_element_type=jnp.float32)
    column = to_column(as_row(mine_ref[pl.ds(piece * LINES, LINES), :]))
    out_ref[0] = column * total[:, 0:E] + total[:, E : 2 * E] - 2.0 * match_ref[...]


def finish_kernel(embed_ref, parts_ref, out_ref):
    x = embed_ref[...]
    inverse = lax.rsqrt(jnp.sum(x * x, axis=1, keepdims=True) + 1e-06)
    unit = x * inverse
    total = parts_ref[0]
    for i in range(1, N_X):
        total = total + parts_ref[i]
    direction = INVERSE_TAU * total
    out_ref[...] = inverse * (direction - unit * jnp.sum(unit * direction, axis=1, keepdims=True))


def f32(*shape):
    return jax.ShapeDtypeStruct(shape, jnp.float32)


def bf16(*shape):
    return jax.ShapeDtypeStruct(shape, jnp.bfloat16)


def exchange(value, axes):
    return lax.all_to_all(value, axes, 0, 0, tiled=True)


def call(kernel, out_shape, *args, specs=None, **more):
    several = isinstance(out_shape, tuple)
    return pl.pallas_call(
        kernel,
        out_shape=out_shape,
        in_specs=specs or [whole] * len(args),
        out_specs=more.pop("out_specs", (whole,) * len(out_shape) if several else whole),
        compiler_params=pltpu.CompilerParams(vmem_limit_bytes=VMEM),
        **more,
    )(*args)


def cost(keys):
    pairs = N_X * R * keys
    return pl.CostEstimate(flops=2 * pairs * E, bytes_accessed=2 * pairs, transcendentals=pairs)


def rows(width):
    return pl.BlockSpec((R, width), lambda g: (g, 0))


def leading(*shape):
    return pl.BlockSpec((1,) + shape, lambda g: (g,) + (0,) * len(shape))


def body(embed, partner, plan):
    far = ROUNDS * GATHERED
    with jax.named_scope("normalize"):
        rounded, sent = call(
            normalize_kernel, (bf16(R, E), bf16(N_X, SENT, E)), embed, partner.reshape(LINES, E)
        )
    with jax.named_scope("queries"):
        queries = exchange(sent, "x")
    with jax.named_scope("own"):
        keys = lax.all_gather(rounded, "zh", axis=0, tiled=True)
    with jax.named_scope("opponents"):
        chunks = exchange(keys.reshape(N_BLOCK, CHUNK, E), BLOCK)
        chosen = call(select_kernel, bf16(N_BLOCK, ROUNDS, CHUNK, E), plan, chunks, queries,
            specs=[smem, whole, pl.BlockSpec(memory_space=pl.ANY)])
        others = exchange(chosen, BLOCK)
    with jax.named_scope("own"):
        own_exps, match, own_sums = call(
            own_kernel,
            (bf16(N_X * R, GATHERED), f32(N_X * R, E), f32(N_X, 8, R)),
            queries,
            keys,
            specs=[leading(SENT, E), whole],
            out_specs=(rows(GATHERED), rows(E), leading(8, R)),
            grid=(N_X,),
            cost_estimate=cost(GATHERED),
        )
    with jax.named_scope("others"):
        exps, line = call(
            others_kernel,
            (bf16(N_X * R, far), f32(N_BLOCK, 16, E)),
            queries,
            others,
            own_sums,
            specs=[leading(SENT, E), whole, leading(8, R)],
            out_specs=(rows(far), pl.BlockSpec((N_BLOCK, 16, E), lambda g: (0, 0, 0))),
            grid=(N_X,),
            cost_estimate=cost(far),
        )
    with jax.named_scope("sums"):
        line = exchange(line, PLANE)
        level, mine, log_partition = call(
            sums_kernel,
            (bf16(N_ZH * N_ZL, 32, E), f32(16, E), f32(LINES, E)),
            line,
            scratch_shapes=[pltpu.VMEM((NEAR, 2, 16, E), jnp.float32)],
        )
        level = exchange(level, COLUMN)
        loss = jnp.sum(level[:, LOSS : LOSS + 3, 0].astype(jnp.float32)) / (N_BLOCK * BLOCK_ROWS)
    with jax.named_scope("direction"):
        parts = call(
            direction_kernel,
            f32(N_X, R, E),
            plan,
            own_exps,
            exps,
            keys,
            others,
            match,
            mine,
            level,
            specs=[smem, rows(GATHERED), rows(far), whole, whole, rows(E), whole, whole],
            scratch_shapes=[
                pltpu.VMEM((N_ZH * N_ZL, 32, E), jnp.float32),
                pltpu.VMEM((GATHERED + far, 2 * E), jnp.bfloat16),
            ],
            out_specs=leading(R, E),
            grid=(N_X,),
            cost_estimate=cost(GATHERED + far),
        )
        parts = exchange(parts, "x")
    with jax.named_scope("finish"):
        grad = call(finish_kernel, f32(R, E), embed, parts)
    return (grad, log_partition.reshape(R), loss)


def solution(mesh):
    split = Mesh(mesh.devices.reshape(SIZES), AXES)
    return jax.shard_map(
        body,
        mesh=split,
        in_specs=(P(AXES, None), P(AXES), P()),
        out_specs=(P(AXES, None), P(AXES), P()),
        check_vma=False,
    )
```

time: 518 us -> 162 us (0.31)
  the two profiles are of different devices: /device:TPU:1 before, /device:TPU:32 now
where the time goes in v2:
time: 162 us; the launch traced here: 161 us
  blocking collectives  86.6 us (53%)
  Pallas kernels  33.2 us (20%)
  waiting for transfers between devices  23 us (14%)
  starting transfers between devices  12.8 us (8%)
  between operations  2.45 us (2%)
  local copies, waits for them, and re-layouts  1.78 us (1%)
    all_to_all x3, blocking collectives, exchange(): return lax.all_to_all(value, axes, 0, 0, tiled=True)  57.6 us
    pallas_call x7, Pallas kernels, call(): pl.pallas_call(kernel, out_shape=out_shape, in_specs=specs or [whole] * l...  33.2 us
    all_gather x1, blocking collectives, body(): keys = lax.all_gather(rounded, 'zh', axis=0, tiled=True)  29 us
    all_to_all x3, waiting for transfers between devices, exchange(): return lax.all_to_all(value, axes, 0, 0, tiled=True)  23 us
    all_to_all x3, starting transfers between devices, exchange(): return lax.all_to_all(value, axes, 0, 0, tiled=True)  12.8 us
  transfers between devices with their start and end apart: 3, of which 2 were waited for; matrix products, arithmetic and copies ran while one was open for 1% of the time, Pallas kernels for 5%

profile of v2, /device:TPU:32, one launch (start us, length us, event | category | flops | bytes accessed | tf_op | source)
XLA Modules:
  0.0 161.1 jit_solution(13733448687085144887)
XLA Ops:
  0.6 1.8 %normalize.1 = (bf16[384,128]{1,0:T(8,128)(2,1)}, bf16[4,400,128]{2,1,0:T(8,128)(2,1)}) custom-call(f32[384,128]{1,0:T(8,128)} %embed_ref.3, s32[3,128]{1,0:T(4,128)} %bitcast.4), custom_call_target="tpu_custom_call" | custom-call | tf_op jit(solution)/shard_map/normalize/pallas_call | solution.py:225
  2.5 4.3 %all-to-all-start = ((bf16[4,400,128]{2,1,0:T(8,128)(2,1)}), bf16[4,400,128]{2,1,0:T(8,128)(2,1)S(1)}, u32[]{:S(2)}, u32[]{:S(2)}) async-start(bf16[4,400,128]{2,1,0:T(8,128)(2,1)} %get-tuple-element.13), calls=%async_computation | async-start | bytes 819200 | tf_op jit(solution)/shard_map/queries/all_to_all | solution.py:220
  6.8 29.0 %all_gather.3.keys_ref = bf16[1536,128]{1,0:T(8,128)(2,1)S(1)} all-gather(bf16[384,128]{1,0:T(8,128)(2,1)} %get-tuple-element.14), channel_id=1, replica_groups=mesh['zl'=4,'y'=4,'c'=2,'x'=4,'zh'=4] {'zh'}, dimensions={0}, use_global_device_ids=true | all-gather | bytes 491520 | tf_op jit(solution)/shard_map/own/all_gather | solution.py:257
  35.8 0.0 copy-start
  35.8 0.0 all-to-all-done.queries_ref
  35.8 0.0 copy-start.3
  35.8 20.1 %all_to_all.30.chunks_ref = bf16[32,48,128]{2,1,0:T(8,128)(2,1)} all-to-all(bf16[32,48,128]{2,1,0:T(8,128)(2,1)S(1)} %bitcast.3), channel_id=1, replica_groups=mesh['zl'=4,'y'=4,'c'=2,'x'=4,'zh'=4] {'zl','y','c'}, dimensions={0} | all-to-all | bytes 786432 | tf_op jit(solution)/shard_map/opponents/all_to_all | solution.py:220
  55.8 0.0 copy-done.3
  55.8 2.0 %opponents.1 = bf16[32,2,48,128]{3,2,1,0:T(8,128)(2,1)} custom-call(s32[2,32]{1,0:T(2,128)} %plan_ref.3, bf16[32,48,128]{2,1,0:T(8,128)(2,1)} %all_to_all.30.chunks_ref, bf16[4,400,128]{2,1,0:T(8,128)(2,1)} %copy-done.3), custom_call_target="tpu_custom_call" | custom-call | tf_op jit(solution)/shard_map/opponents/pallas_call | solution.py:225
  57.8 5.0 %all-to-all-start.2 = ((bf16[32,2,48,128]{3,2,1,0:T(8,128)(2,1)}), bf16[32,2,48,128]{3,2,1,0:T(8,128)(2,1)S(1)}, u32[]{:S(2)}, u32[]{:S(2)}) async-start(bf16[32,2,48,128]{3,2,1,0:T(8,128)(2,1)} %opponents.1), calls=%async_computation.2 | async-start | bytes 1572864 | tf_op jit(solution)/shard_map/opponents/all_to_all | solution.py:220
  62.8 0.0 copy-done
  62.8 7.4 %own.1 = (bf16[1536,1536]{1,0:T(8,128)(2,1)}, f32[1536,128]{1,0:T(8,128)}, f32[4,8,384]{2,1,0:T(8,128)}) custom-call(bf16[4,400,128]{2,1,0:T(8,128)(2,1)} %copy-done.3, bf16[1536,128]{1,0:T(8,128)(2,1)} %copy-done), custom_call_target="tpu_custom_call" | custom-call | flops 603979776 | bytes 4718592 | tf_op jit(solution)/shard_map/own/pallas_call | solution.py:225
  70.2 13.0 %all-to-all-done.2.keys_ref.far_ref = bf16[32,2,48,128]{3,2,1,0:T(8,128)(2,1)S(1)} async-done(((bf16[32,2,48,128]{3,2,1,0:T(8,128)(2,1)}), bf16[32,2,48,128]{3,2,1,0:T(8,128)(2,1)S(1)}, u32[]{:S(2)}, u32[]{:S(2)}) %all-to-all-start.2) | async-done | bytes 786464 | tf_op jit(solution)/shard_map/opponents/all_to_all | solution.py:220
  83.3 0.9 copy-done.1
  84.1 7.9 %others.1 = (bf16[1536,3072]{1,0:T(8,128)(2,1)}, f32[32,16,128]{2,1,0:T(8,128)}) custom-call(bf16[4,400,128]{2,1,0:T(8,128)(2,1)} %copy-done.3, bf16[32,2,48,128]{3,2,1,0:T(8,128)(2,1)} %copy-done.1, f32[4,8,384]{2,1,0:T(8,128)} %get-tuple-element.16.own_ref), custom_call_target="tpu_custom_call" | custom-call | flops 1207959552 | bytes 9437184 | tf_op jit(solution)/shard_map/others/pallas_call | solution.py:225
  92.1 15.1 %all_to_all.31.line_ref = f32[32,16,128]{2,1,0:T(8,128)} all-to-all(f32[32,16,128]{2,1,0:T(8,128)} %get-tuple-element.19), channel_id=1, replica_groups=mesh['zl'=4,'y'=4,'c'=2,'x'=4,'zh'=4] {'y','x','c'}, dimensions={0} | all-to-all | bytes 524288 | tf_op jit(solution)/shard_map/sums/all_to_all | solution.py:220
  107.2 1.8 %sums.1 = (bf16[16,32,128]{2,1,0:T(8,128)(2,1)}, f32[16,128]{1,0:T(8,128)}, f32[3,128]{1,0:T(4,128)}) custom-call(f32[32,16,128]{2,1,0:T(8,128)} %all_to_all.31.line_ref), custom_call_target="tpu_custom_call" | custom-call | tf_op jit(solution)/shard_map/sums/pallas_call | solution.py:225
  108.9 22.4 %all_to_all.32.sums_ref = bf16[16,32,128]{2,1,0:T(8,128)(2,1)} all-to-all(bf16[16,32,128]{2,1,0:T(8,128)(2,1)} %get-tuple-element.21), channel_id=1, replica_groups=mesh['zl'=4,'y'=4,'c'=2,'x'=4,'zh'=4] {'zh','zl'}, dimensions={0} | all-to-all | bytes 262144 | tf_op jit(solution)/shard_map/sums/all_to_all | solution.py:220
  131.3 10.1 %direction.1 = f32[4,384,128]{2,1,0:T(8,128)} custom-call(s32[2,32]{1,0:T(2,128)} %plan_ref.3, bf16[1536,1536]{1,0:T(8,128)(2,1)} %get-tuple-element.15.own_ref, bf16[1536,3072]{1,0:T(8,128)(2,1)} %get-tuple-element.17.others_ref, bf16[1536,128]{1,0:T(8,128)(2,1)} %copy-done, bf16[32,2,48,128]{3,2,1,0:T(8,128)(2,1)} %copy-done.1, ...), custom_call_target="tpu_custom_call" | custom-call | flops 1811939328 | bytes 14155776 | tf_op jit(solution)/shard_map/direction/pallas_call | solution.py:225
  141.5 3.5 %all-to-all-start.5 = ((f32[4,384,128]{2,1,0:T(8,128)}), f32[4,384,128]{2,1,0:T(8,128)S(1)}, u32[]{:S(2)}, u32[]{:S(2)}) async-start(f32[4,384,128]{2,1,0:T(8,128)} %direction.1), calls=%async_computation.5 | async-start | bytes 1572864 | tf_op jit(solution)/shard_map/direction/all_to_all | solution.py:220
  145.0 1.4 convert_reduce_fusion
  147.0 10.0 %all-to-all-done.5.parts_ref = f32[4,384,128]{2,1,0:T(8,128)S(1)} async-done(((f32[4,384,128]{2,1,0:T(8,128)}), f32[4,384,128]{2,1,0:T(8,128)S(1)}, u32[]{:S(2)}, u32[]{:S(2)}) %all-to-all-start.5) | async-done | bytes 786464 | tf_op jit(solution)/shard_map/direction/all_to_all | solution.py:220
  157.0 0.9 copy-done.2
  157.9 2.1 %finish.1 = f32[384,128]{1,0:T(8,128)} custom-call(f32[384,128]{1,0:T(8,128)} %embed_ref.3, f32[4,384,128]{2,1,0:T(8,128)} %copy-done.2), custom_call_target="tpu_custom_call" | custom-call | tf_op jit(solution)/shard_map/finish/pallas_call | solution.py:225
  (2 shorter events, 0.0 us)
Async XLA Ops:
  2.5 33.3 %all-to-all-start = ((bf16[4,400,128]{2,1,0:T(8,128)(2,1)}), bf16[4,400,128]{2,1,0:T(8,128)(2,1)S(1)}, u32[]{:S(2)}, u32[]{:S(2)}) async-start(bf16[4,400,128]{2,1,0:T(8,128)(2,1)} %get-tuple-element.13), calls=%async_computation | async-start | bytes 819200 | tf_op jit(solution)/shard_map/queries/all_to_all | solution.py:220
  35.8 27.1 %copy-start = (bf16[1536,128]{1,0:T(8,128)(2,1)}, bf16[1536,128]{1,0:T(8,128)(2,1)S(1)}, u32[]{:S(2)}) copy-start(bf16[1536,128]{1,0:T(8,128)(2,1)S(1)} %all_gather.3.keys_ref) | copy-start | bytes 1179652
  35.8 20.1 %copy-start.3 = (bf16[4,400,128]{2,1,0:T(8,128)(2,1)}, bf16[4,400,128]{2,1,0:T(8,128)(2,1)S(1)}, u32[]{:S(2)}) copy-start(bf16[4,400,128]{2,1,0:T(8,128)(2,1)S(1)} %all-to-all-done.queries_ref) | copy-start | bytes 1228804
  57.8 25.5 %all-to-all-start.2 = ((bf16[32,2,48,128]{3,2,1,0:T(8,128)(2,1)}), bf16[32,2,48,128]{3,2,1,0:T(8,128)(2,1)S(1)}, u32[]{:S(2)}, u32[]{:S(2)}) async-start(bf16[32,2,48,128]{3,2,1,0:T(8,128)(2,1)} %opponents.1), calls=%async_computation.2 | async-start | bytes 1572864 | tf_op jit(solution)/shard_map/opponents/all_to_all | solution.py:220
  83.3 0.9 copy-start.1
  141.5 15.5 %all-to-all-start.5 = ((f32[4,384,128]{2,1,0:T(8,128)}), f32[4,384,128]{2,1,0:T(8,128)S(1)}, u32[]{:S(2)}, u32[]{:S(2)}) async-start(f32[4,384,128]{2,1,0:T(8,128)} %direction.1), calls=%async_computation.5 | async-start | bytes 1572864 | tf_op jit(solution)/shard_map/direction/all_to_all | solution.py:220
  157.0 0.9 copy-start.2

commit v3 on v2

v3 whole, which is shorter than its diff:
```python
import jax
import jax.numpy as jnp
import numpy as np
from jax import lax
from jax.experimental import pallas as pl
from jax.experimental.pallas import tpu as pltpu
from jax.sharding import Mesh
from jax.sharding import PartitionSpec as P

ROUNDS = 2
INVERSE_TAU = 10.0
SCALE = INVERSE_TAU * float(np.log2(np.e))

AXES = ("zl", "y", "c", "x", "zh")
SIZES = (4, 4, 2, 4, 4)
BLOCK = ("zl", "y", "c")
PLANE = ("y", "x", "c")
COLUMN = ("zh", "zl")

R = 384
E = 128
N_BLOCK = 32
N_X = 4
N_ZL = 4
N_ZH = 4
GATHERED = R * N_ZH
BLOCK_ROWS = GATHERED * N_X
CHUNK = GATHERED // N_BLOCK
SENT = R + 16
LINES = R // E
SLOT = LINES * N_X
NEAR = 8
LOSS = LINES * NEAR
VMEM = 12 * 1024 * 1024

whole = pl.BlockSpec(memory_space=pltpu.VMEM)
smem = pl.BlockSpec(memory_space=pltpu.SMEM)
anywhere = pl.BlockSpec(memory_space=pl.ANY)


def as_row(lines):
    return jnp.concatenate([lines[i : i + 1] for i in range(LINES)], axis=1)


def as_lines(row):
    return jnp.concatenate([row[0:1, i * E : (i + 1) * E] for i in range(LINES)], axis=0)


def to_column(row):
    return jnp.transpose(jnp.broadcast_to(row, (E, R)))


def widen(wide):
    return jnp.concatenate([wide] * LINES, axis=1)


def lane_sums(value):
    return jnp.sum(jnp.transpose(value), axis=0, keepdims=True)


def scores(q, k):
    return lax.dot_general(q, k, (((1,), (1,)), ((), ())), preferred_element_type=jnp.float32)


def fold(e):
    part = e[:, 0:E]
    for i in range(1, LINES):
        part = part + e[:, i * E : (i + 1) * E]
    return part


def far_keys(keys_ref, t, z):
    each = R // CHUNK
    return jnp.concatenate([keys_ref[z * each + i, t] for i in range(each)], axis=0)


def normalize_kernel(embed_ref, partner_ref, rounded_ref, sent_ref):
    x = embed_ref[...]
    inverse = lax.rsqrt(jnp.sum(x * x, axis=1, keepdims=True) + 1e-06)
    rounded = (x * inverse).astype(jnp.bfloat16)
    rounded_ref[...] = rounded
    index = partner_ref[...]
    high = index // 128
    low = index - high * 128
    both = jnp.concatenate([high, low, jnp.zeros((16 - 2 * LINES, E), jnp.int32)], axis=0)
    index = both.astype(jnp.float32).astype(jnp.bfloat16)
    for xp in range(N_X):
        sent_ref[xp, 0:R] = rounded
        sent_ref[xp, R:SENT] = index


def select_kernel(plan_ref, chunks_ref, queries_ref, out_ref):
    for b in range(N_BLOCK):
        for t in range(ROUNDS):
            out_ref[b, t] = chunks_ref[plan_ref[t, b]]


def own_kernel(queries_ref, keys_ref, exp_ref, match_ref, total_ref):
    x = lax.axis_index("x")
    zh = lax.axis_index("zh")
    lane = lax.broadcasted_iota(jnp.int32, (R, R), 1)
    itself = lax.broadcasted_iota(jnp.int32, (R, R), 0) - lane
    for piece in range(N_X):
        q = queries_ref[piece, 0:R]
        rows = slice(piece * R, (piece + 1) * R)
        index = queries_ref[piece, R:SENT].astype(jnp.float32)
        index = as_row(index[0:LINES]) * 128.0 + as_row(index[LINES : 2 * LINES])
        partner = widen(to_column(index)).astype(jnp.int32) - x * GATHERED - lane
        for z in range(N_ZH):
            k = keys_ref[z * R : (z + 1) * R]
            e = jnp.exp2(scores(q, k) * SCALE - SCALE)
            e = jnp.where(itself == (x - piece) * GATHERED + (z - zh) * R, 0.0, e)
            exp_ref[rows, z * R : (z + 1) * R] = e.astype(jnp.bfloat16)
            chosen = jnp.where(partner == z * R, 1.0, 0.0).astype(jnp.bfloat16)
            match = jnp.dot(chosen, k, preferred_element_type=jnp.float32)
            part = fold(e)
            if z > 0:
                match = match + match_ref[rows]
                part = part + total_ref[rows]
            match_ref[rows] = match
            total_ref[rows] = part


def others_kernel(queries_ref, keys_ref, match_ref, own_ref, exp_ref, line_ref, total):
    for t in range(ROUNDS):
        for z in range(N_ZH):
            k = far_keys(keys_ref, t, z)
            at = (t * N_ZH + z) * R
            for piece in range(N_X):
                rows = slice(piece * R, (piece + 1) * R)
                e = jnp.exp2(scores(queries_ref[piece, 0:R], k) * SCALE - SCALE)
                exp_ref[rows, at : at + R] = e.astype(jnp.bfloat16)
                total[rows] = fold(e) + (total[rows] if at > 0 else own_ref[rows])
    sums = lane_sums(total[...])
    lines = [sums[0:1, i * E : (i + 1) * E] for i in range(N_X * LINES)]
    positive = jnp.zeros((8, E), jnp.float32)
    for piece in range(N_X):
        match = match_ref[piece * R : (piece + 1) * R] * queries_ref[piece, 0:R].astype(jnp.float32)
        positive = positive + jnp.sum(match.reshape(R // 8, 8, E), axis=0)
    positive = jnp.sum(positive, axis=(0, 1), keepdims=True)
    lines = jnp.concatenate(lines + [jnp.broadcast_to(positive, (16 - SLOT, E))], axis=0)
    for i in range(N_BLOCK):
        line_ref[i] = lines


def sums_kernel(line_ref, level_ref, mine_ref, log_ref, held):
    near = lax.axis_index("y") * 2 + lax.axis_index("c")
    x = lax.axis_index("x")
    slot = lax.broadcasted_iota(jnp.int32, (16, E), 0)
    loss = jnp.zeros((16, E), jnp.float32)
    for i in range(NEAR):
        y, c = divmod(i, 2)
        part = line_ref[y * 8 + c]
        for j in range(1, N_X):
            part = part + line_ref[y * 8 + j * 2 + c]
        sums = jnp.where(slot < SLOT, part, 1.0)
        logs = INVERSE_TAU + jnp.log(sums)
        loss = loss + jnp.where(slot < SLOT, logs, 0.0)
        loss = loss - jnp.where(slot == SLOT, part * (INVERSE_TAU / E), 0.0)
        held[i, 0] = 1.0 / sums
        held[i, 1] = logs
    mine_ref[...] = held[near, 0]
    log_ref[...] = held[near, 1, pl.ds(x * LINES, LINES), :]
    level = [held[i, 0, pl.ds(x * LINES, LINES), :] for i in range(NEAR)]
    loss = jnp.broadcast_to(jnp.sum(loss, axis=(0, 1), keepdims=True), (1, E))
    for _ in range(3):
        level.append(loss.astype(jnp.bfloat16).astype(jnp.float32))
        loss = loss - level[-1]
    level.append(jnp.zeros((32 - LOSS - 3, E), jnp.float32))
    level = jnp.concatenate(level, axis=0).astype(jnp.bfloat16)
    for i in range(N_ZH * N_ZL):
        level_ref[i] = level


def direction_kernel(
    plan_ref, own_ref, others_ref, keys_ref, far_ref, match_ref, mine_ref, sums_ref, out_ref, held, both
):
    zl, y, c = (lax.axis_index(a) for a in BLOCK)
    here = (zl * 4 + y) * 2 + c
    held[...] = sums_ref[...].astype(jnp.float32)
    for t in range(ROUNDS + 1):
        other = here if t == 0 else plan_ref[t - 1, here]
        level = other // NEAR
        near = other - level * NEAR
        for z in range(N_ZH):
            inverse = to_column(as_row(held[z * N_ZL + level, pl.ds(near * LINES, LINES), :]))
            k = keys_ref[z * R : (z + 1) * R] if t == 0 else far_keys(far_ref, t - 1, z)
            at = (t * N_ZH + z) * R
            both[at : at + R, 0:E] = k
            both[at : at + R, E : 2 * E] = (k.astype(jnp.float32) * inverse).astype(jnp.bfloat16)
    for piece in range(N_X):
        rows = slice(piece * R, (piece + 1) * R)
        total = jnp.dot(own_ref[rows], both[0:GATHERED], preferred_element_type=jnp.float32)
        total = total + jnp.dot(others_ref[rows], both[GATHERED:], preferred_element_type=jnp.float32)
        column = to_column(as_row(mine_ref[piece * LINES : (piece + 1) * LINES, :]))
        out_ref[piece] = column * total[:, 0:E] + total[:, E : 2 * E] - 2.0 * match_ref[rows]


def finish_kernel(embed_ref, parts_ref, out_ref):
    x = embed_ref[...]
    inverse = lax.rsqrt(jnp.sum(x * x, axis=1, keepdims=True) + 1e-06)
    unit = x * inverse
    total = parts_ref[0]
    for i in range(1, N_X):
        total = total + parts_ref[i]
    direction = INVERSE_TAU * total
    out_ref[...] = inverse * (direction - unit * jnp.sum(unit * direction, axis=1, keepdims=True))


def f32(*shape):
    return jax.ShapeDtypeStruct(shape, jnp.float32)


def bf16(*shape):
    return jax.ShapeDtypeStruct(shape, jnp.bfloat16)


def exchange(value, axes):
    return lax.all_to_all(value, axes, 0, 0, tiled=True)


def call(kernel, out_shape, *args, specs=None, **more):
    return pl.pallas_call(
        kernel,
        out_shape=out_shape,
        in_specs=specs or [whole] * len(args),
        out_specs=(whole,) * len(out_shape) if isinstance(out_shape, tuple) else whole,
        compiler_params=pltpu.CompilerParams(vmem_limit_bytes=VMEM),
        **more,
    )(*args)


def cost(keys):
    pairs = N_X * R * keys
    return pl.CostEstimate(flops=2 * pairs * E, bytes_accessed=2 * pairs, transcendentals=pairs)


def body(embed, partner, plan):
    far = ROUNDS * GATHERED
    with jax.named_scope("normalize"):
        rounded, sent = call(
            normalize_kernel, (bf16(R, E), bf16(N_X, SENT, E)), embed, partner.reshape(LINES, E)
        )
    with jax.named_scope("queries"):
        queries = exchange(sent, "x")
    with jax.named_scope("own"):
        keys = lax.all_gather(rounded, "zh", axis=0, tiled=True)
    with jax.named_scope("opponents"):
        chunks = exchange(keys.reshape(N_BLOCK, CHUNK, E), BLOCK)
        chosen = call(select_kernel, bf16(N_BLOCK, ROUNDS, CHUNK, E), plan, chunks, queries,
            specs=[smem, whole, anywhere])
        others = exchange(chosen, BLOCK)
    with jax.named_scope("own"):
        own_exps, match, total = call(
            own_kernel,
            (bf16(N_X * R, GATHERED), f32(N_X * R, E), f32(N_X * R, E)),
            queries,
            keys,
            cost_estimate=cost(GATHERED),
        )
    with jax.named_scope("others"):
        exps, line = call(
            others_kernel,
            (bf16(N_X * R, far), f32(N_BLOCK, 16, E)),
            queries,
            others,
            match,
            total,
            scratch_shapes=[pltpu.VMEM((N_X * R, E), jnp.float32)],
            cost_estimate=cost(far),
        )
    with jax.named_scope("sums"):
        line = exchange(line, PLANE)
        level, mine, log_partition = call(
            sums_kernel,
            (bf16(N_ZH * N_ZL, 32, E), f32(16, E), f32(LINES, E)),
            line,
            scratch_shapes=[pltpu.VMEM((NEAR, 2, 16, E), jnp.float32)],
        )
        level = exchange(level, COLUMN)
        loss = jnp.sum(level[:, LOSS : LOSS + 3, 0].astype(jnp.float32)) / (N_BLOCK * BLOCK_ROWS)
    with jax.named_scope("direction"):
        parts = call(
            direction_kernel,
            f32(N_X, R, E),
            plan,
            own_exps,
            exps,
            keys,
            others,
            match,
            mine,
            level,
            specs=[smem] + [whole] * 7,
            scratch_shapes=[
                pltpu.VMEM((N_ZH * N_ZL, 32, E), jnp.float32),
                pltpu.VMEM((GATHERED + far, 2 * E), jnp.bfloat16),
            ],
            cost_estimate=cost(GATHERED + far),
        )
        parts = exchange(parts, "x")
    with jax.named_scope("finish"):
        grad = call(finish_kernel, f32(R, E), embed, parts)
    return (grad, log_partition.reshape(R), loss)


def solution(mesh):
    split = Mesh(mesh.devices.reshape(SIZES), AXES)
    return jax.shard_map(
        body,
        mesh=split,
        in_specs=(P(AXES, None), P(AXES), P()),
        out_specs=(P(AXES, None), P(AXES), P()),
        check_vma=False,
    )
```

time: 162 us -> 150 us (0.926)
  Pallas kernels: 33.2 us -> 17.2 us
  local copies, waits for them, and re-layouts: 1.78 us -> 4.42 us
  waiting for transfers between devices: 23 us -> 25.5 us
    pallas_call x7, Pallas kernels: 33.2 us -> 17.2 us  [call(): pl.pallas_call(kernel, out_shape=out_shape, in_specs=specs or [whole] * l...]
    unnamed x8 -> x16, local copies, waits for them, and re-layouts: 1.78 us -> 4.42 us
    all_to_all x3, waiting for transfers between devices: 23 us -> 25.5 us  [exchange(): return lax.all_to_all(value, axes, 0, 0, tiled=True)]
  transfers between devices with their start and end apart: 3 -> 3, of which waited for: 2 -> 2; matrix products, arithmetic and copies ran while one was open for 1% -> 0% of each run, Pallas kernels for 5% -> 2%
where the time goes in v3:
time: 150 us; the launch traced here: 149 us
  blocking collectives  85.9 us (57%)
  waiting for transfers between devices  25.5 us (17%)
  Pallas kernels  17.2 us (11%)
  starting transfers between devices  12.8 us (9%)
  local copies, waits for them, and re-layouts  4.42 us (3%)
  between operations  2.48 us (2%)
    all_to_all x3, blocking collectives, exchange(): return lax.all_to_all(value, axes, 0, 0, tiled=True)  57 us
    all_gather x1, blocking collectives, body(): keys = lax.all_gather(rounded, 'zh', axis=0, tiled=True)  28.9 us
    all_to_all x3, waiting for transfers between devices, exchange(): return lax.all_to_all(value, axes, 0, 0, tiled=True)  25.5 us
    pallas_call x7, Pallas kernels, call(): pl.pallas_call(kernel, out_shape=out_shape, in_specs=specs or [whole] * l...  17.2 us
    all_to_all x3, starting transfers between devices, exchange(): return lax.all_to_all(value, axes, 0, 0, tiled=True)  12.8 us
    unnamed x16, local copies, waits for them, and re-layouts  4.42 us
  transfers between devices with their start and end apart: 3, of which 2 were waited for; matrix products, arithmetic and copies ran while one was open for 0% of the time, Pallas kernels for 2%

profile of v3, /device:TPU:32, one launch (start us, length us, event | category | flops | bytes accessed | tf_op | source)
XLA Modules:
  0.0 149.0 jit_solution(15763256445986560884)
XLA Ops:
  0.6 0.0 copy-start.1
  0.6 0.9 copy-done.1
  1.6 0.7 copy-done.5
  2.2 0.9 normalize.1
  3.1 4.3 %all-to-all-start = ((bf16[4,400,128]{2,1,0:T(8,128)(2,1)}), bf16[4,400,128]{2,1,0:T(8,128)(2,1)S(1)}, u32[]{:S(2)}, u32[]{:S(2)}) async-start(bf16[4,400,128]{2,1,0:T(8,128)(2,1)} %get-tuple-element.13), calls=%async_computation | async-start | bytes 819200 | tf_op jit(solution)/shard_map/queries/all_to_all | solution.py:219
  7.4 28.9 %all_gather.3.keys_ref = bf16[1536,128]{1,0:T(8,128)(2,1)S(1)} all-gather(bf16[384,128]{1,0:T(8,128)(2,1)S(1)} %get-tuple-element.14), channel_id=1, replica_groups=mesh['zl'=4,'y'=4,'c'=2,'x'=4,'zh'=4] {'zh'}, dimensions={0}, use_global_device_ids=true | all-gather | bytes 491520 | tf_op jit(solution)/shard_map/own/all_gather | solution.py:247
  36.3 0.0 all-to-all-done.queries_ref
  36.3 20.0 %all_to_all.30.chunks_ref = bf16[32,48,128]{2,1,0:T(8,128)(2,1)S(1)} all-to-all(bf16[32,48,128]{2,1,0:T(8,128)(2,1)S(1)} %bitcast.5), channel_id=1, replica_groups=mesh['zl'=4,'y'=4,'c'=2,'x'=4,'zh'=4] {'zl','y','c'}, dimensions={0} | all-to-all | bytes 786432 | tf_op jit(solution)/shard_map/opponents/all_to_all | solution.py:219
  56.3 0.7 copy-done.3
  57.0 1.5 %opponents.1 = bf16[32,2,48,128]{3,2,1,0:T(8,128)(2,1)} custom-call(s32[2,32]{1,0:T(2,128)S(1)} %copy-done.3, bf16[32,48,128]{2,1,0:T(8,128)(2,1)S(1)} %all_to_all.30.chunks_ref, bf16[4,400,128]{2,1,0:T(8,128)(2,1)S(1)} %all-to-all-done.queries_ref), custom_call_target="tpu_custom_call" | custom-call | tf_op jit(solution)/shard_map/opponents/pallas_call | solution.py:223
  58.5 5.0 %all-to-all-start.2 = ((bf16[32,2,48,128]{3,2,1,0:T(8,128)(2,1)}), bf16[32,2,48,128]{3,2,1,0:T(8,128)(2,1)S(1)}, u32[]{:S(2)}, u32[]{:S(2)}) async-start(bf16[32,2,48,128]{3,2,1,0:T(8,128)(2,1)} %opponents.1), calls=%async_computation.2 | async-start | bytes 1572864 | tf_op jit(solution)/shard_map/opponents/all_to_all | solution.py:219
  63.5 3.5 %own.1 = (bf16[1536,1536]{1,0:T(8,128)(2,1)S(1)}, f32[1536,128]{1,0:T(8,128)S(1)}, f32[1536,128]{1,0:T(8,128)S(1)}) custom-call(bf16[4,400,128]{2,1,0:T(8,128)(2,1)S(1)} %all-to-all-done.queries_ref, bf16[1536,128]{1,0:T(8,128)(2,1)S(1)} %all_gather.3.keys_ref), custom_call_target="tpu_custom_call" | custom-call | flops 603979776 | bytes 4718592 | tf_op jit(solution)/shard_map/own/pallas_call | solution.py:223
  67.0 2.1 %copy-done = bf16[1536,1536]{1,0:T(8,128)(2,1)} copy-done((bf16[1536,1536]{1,0:T(8,128)(2,1)}, bf16[1536,1536]{1,0:T(8,128)(2,1)S(1)}, u32[]{:S(2)}) %copy-start) | copy-done | bytes 4718616
  69.1 14.8 %all-to-all-done.2.keys_ref.far_ref = bf16[32,2,48,128]{3,2,1,0:T(8,128)(2,1)S(1)} async-done(((bf16[32,2,48,128]{3,2,1,0:T(8,128)(2,1)}), bf16[32,2,48,128]{3,2,1,0:T(8,128)(2,1)S(1)}, u32[]{:S(2)}, u32[]{:S(2)}) %all-to-all-start.2) | async-done | bytes 786464 | tf_op jit(solution)/shard_map/opponents/all_to_all | solution.py:219
  84.0 4.3 %others.1 = (bf16[1536,3072]{1,0:T(8,128)(2,1)S(1)}, f32[32,16,128]{2,1,0:T(8,128)S(1)}) custom-call(bf16[4,400,128]{2,1,0:T(8,128)(2,1)S(1)} %all-to-all-done.queries_ref, bf16[32,2,48,128]{3,2,1,0:T(8,128)(2,1)S(1)} %all-to-all-done.2.keys_ref.far_ref, f32[1536,128]{1,0:T(8,128)S(1)} %get-tuple-element.16.match_ref, f32[1536,128]{1,0:T(8,128)S(1)} %get-tuple-element.17.own_ref), custom_call_target="tpu_custom_call" | custom-call | flops 1207959552 | bytes 9437184 | tf_op jit(solution)/shard_map/others/pallas_call | solution.py:223
  88.2 14.8 %all_to_all.31.line_ref = f32[32,16,128]{2,1,0:T(8,128)S(1)} all-to-all(f32[32,16,128]{2,1,0:T(8,128)S(1)} %get-tuple-element.19), channel_id=1, replica_groups=mesh['zl'=4,'y'=4,'c'=2,'x'=4,'zh'=4] {'y','x','c'}, dimensions={0} | all-to-all | bytes 524288 | tf_op jit(solution)/shard_map/sums/all_to_all | solution.py:219
  103.0 0.6 sums.1
  103.6 22.3 %all_to_all.32.sums_ref = bf16[16,32,128]{2,1,0:T(8,128)(2,1)S(1)} all-to-all(bf16[16,32,128]{2,1,0:T(8,128)(2,1)S(1)} %get-tuple-element.21), channel_id=1, replica_groups=mesh['zl'=4,'y'=4,'c'=2,'x'=4,'zh'=4] {'zh','zl'}, dimensions={0} | all-to-all | bytes 262144 | tf_op jit(solution)/shard_map/sums/all_to_all | solution.py:219
  125.9 0.0 copy-done.4
  125.9 5.5 %direction.1 = f32[4,384,128]{2,1,0:T(8,128)} custom-call(s32[2,32]{1,0:T(2,128)S(1)} %copy-done.4, bf16[1536,1536]{1,0:T(8,128)(2,1)S(1)} %bitcast.4, bf16[1536,3072]{1,0:T(8,128)(2,1)S(1)} %get-tuple-element.18.others_ref, bf16[1536,128]{1,0:T(8,128)(2,1)S(1)} %all_gather.3.keys_ref, bf16[32,2,48,128]{3,2,1,0:T(8,128)(2,1)S(1)} %all-to-all-done.2.keys_ref.far_ref, ...), custom_call_target="tpu_custom_call" | custom-call | flops 1811939328 | bytes 14155776 | tf_op jit(solution)/shard_map/direction/pallas_call | solution.py:223
  131.4 3.5 %all-to-all-start.5 = ((f32[4,384,128]{2,1,0:T(8,128)}), f32[4,384,128]{2,1,0:T(8,128)S(1)}, u32[]{:S(2)}, u32[]{:S(2)}) async-start(f32[4,384,128]{2,1,0:T(8,128)} %direction.1), calls=%async_computation.5 | async-start | bytes 1572864 | tf_op jit(solution)/shard_map/direction/all_to_all | solution.py:219
  134.9 0.6 convert_reduce_fusion
  136.2 10.7 %all-to-all-done.5.parts_ref = f32[4,384,128]{2,1,0:T(8,128)S(1)} async-done(((f32[4,384,128]{2,1,0:T(8,128)}), f32[4,384,128]{2,1,0:T(8,128)S(1)}, u32[]{:S(2)}, u32[]{:S(2)}) %all-to-all-start.5) | async-done | bytes 786464 | tf_op jit(solution)/shard_map/direction/all_to_all | solution.py:219
  147.0 0.9 finish.1
  (11 shorter events, 0.0 us)
Async XLA Ops:
  0.6 0.9 copy-start.1
  1.6 0.7 copy-start.5
  3.1 33.2 %all-to-all-start = ((bf16[4,400,128]{2,1,0:T(8,128)(2,1)}), bf16[4,400,128]{2,1,0:T(8,128)(2,1)S(1)}, u32[]{:S(2)}, u32[]{:S(2)}) async-start(bf16[4,400,128]{2,1,0:T(8,128)(2,1)} %get-tuple-element.13), calls=%async_computation | async-start | bytes 819200 | tf_op jit(solution)/shard_map/queries/all_to_all | solution.py:219
  7.4 118.5 %copy-start.4 = (s32[2,32]{1,0:T(2,128)S(1)}, s32[2,32]{1,0:T(2,128)}, u32[]{:S(2)}) copy-start(s32[2,32]{1,0:T(2,128)} %plan_ref.3) | copy-start | bytes 772
  56.3 0.7 copy-start.3
  58.5 25.5 %all-to-all-start.2 = ((bf16[32,2,48,128]{3,2,1,0:T(8,128)(2,1)}), bf16[32,2,48,128]{3,2,1,0:T(8,128)(2,1)S(1)}, u32[]{:S(2)}, u32[]{:S(2)}) async-start(bf16[32,2,48,128]{3,2,1,0:T(8,128)(2,1)} %opponents.1), calls=%async_computation.2 | async-start | bytes 1572864 | tf_op jit(solution)/shard_map/opponents/all_to_all | solution.py:219
  67.0 2.1 %copy-start = (bf16[1536,1536]{1,0:T(8,128)(2,1)}, bf16[1536,1536]{1,0:T(8,128)(2,1)S(1)}, u32[]{:S(2)}) copy-start(bf16[1536,1536]{1,0:T(8,128)(2,1)S(1)} %get-tuple-element.15.own_ref) | copy-start | bytes 14155780
  83.9 41.9 %slice-start = ((s8[4718592]{0:T(1024)(128)(4,1)}), s8[4194304]{0:T(1024)(128)(4,1)S(1)}, s32[]{:S(2)}) async-start(s8[4718592]{0:T(1024)(128)(4,1)} %bitcast.3), calls=%async_computation.6 | async-start | bytes 8388608
  84.0 41.9 %slice-start.1 = ((s8[4718592]{0:T(1024)(128)(4,1)}), s8[524288]{0:T(1024)(128)(4,1)S(1)}, s32[]{:S(2)}) async-start(s8[4718592]{0:T(1024)(128)(4,1)} %bitcast.3), calls=%async_computation.7 | async-start | bytes 1048576
  103.6 43.3 %copy-start.2 = (f32[384,128]{1,0:T(8,128)S(1)}, f32[384,128]{1,0:T(8,128)}, u32[]{:S(2)}) copy-start(f32[384,128]{1,0:T(8,128)} %embed_ref.3) | copy-start | bytes 589828
  131.4 15.5 %all-to-all-start.5 = ((f32[4,384,128]{2,1,0:T(8,128)}), f32[4,384,128]{2,1,0:T(8,128)S(1)}, u32[]{:S(2)}, u32[]{:S(2)}) async-start(f32[4,384,128]{2,1,0:T(8,128)} %direction.1), calls=%async_computation.5 | async-start | bytes 1572864 | tf_op jit(solution)/shard_map/direction/all_to_all | solution.py:219

commit v4 on v3

--- a/solution.py
+++ b/solution.py
@@ -35,7 +35,6 @@
 
 whole = pl.BlockSpec(memory_space=pltpu.VMEM)
 smem = pl.BlockSpec(memory_space=pltpu.SMEM)
-anywhere = pl.BlockSpec(memory_space=pl.ANY)
 
 
 def as_row(lines):
@@ -84,22 +83,22 @@
     low = index - high * 128
     both = jnp.concatenate([high, low, jnp.zeros((16 - 2 * LINES, E), jnp.int32)], axis=0)
     index = both.astype(jnp.float32).astype(jnp.bfloat16)
-    for xp in range(N_X):
-        sent_ref[xp, 0:R] = rounded
-        sent_ref[xp, R:SENT] = index
-
-
-def select_kernel(plan_ref, chunks_ref, queries_ref, out_ref):
+    sent_ref[0:R] = rounded
+    sent_ref[R:SENT] = index
+
+
+def select_kernel(plan_ref, chunks_ref, out_ref):
     for b in range(N_BLOCK):
         for t in range(ROUNDS):
             out_ref[b, t] = chunks_ref[plan_ref[t, b]]
 
 
-def own_kernel(queries_ref, keys_ref, exp_ref, match_ref, total_ref):
+def own_kernel(queries_ref, keys_ref, exp_ref, match_ref, total_ref, positive_ref):
     x = lax.axis_index("x")
     zh = lax.axis_index("zh")
     lane = lax.broadcasted_iota(jnp.int32, (R, R), 1)
     itself = lax.broadcasted_iota(jnp.int32, (R, R), 0) - lane
+    positive = jnp.zeros((8, E), jnp.float32)
     for piece in range(N_X):
         q = queries_ref[piece, 0:R]
         rows = slice(piece * R, (piece + 1) * R)
@@ -119,9 +118,12 @@
                 part = part + total_ref[rows]
             match_ref[rows] = match
             total_ref[rows] = part
-
-
-def others_kernel(queries_ref, keys_ref, match_ref, own_ref, exp_ref, line_ref, total):
+        match = match * q.astype(jnp.float32)
+        positive = positive + jnp.sum(match.reshape(R // 8, 8, E), axis=0)
+    positive_ref[...] = jnp.broadcast_to(jnp.sum(positive, axis=(0, 1), keepdims=True), (8, E))
+
+
+def others_kernel(queries_ref, keys_ref, positive_ref, own_ref, exp_ref, line_ref, total):
     for t in range(ROUNDS):
         for z in range(N_ZH):
             k = far_keys(keys_ref, t, z)
@@ -133,12 +135,7 @@
                 total[rows] = fold(e) + (total[rows] if at > 0 else own_ref[rows])
     sums = lane_sums(total[...])
     lines = [sums[0:1, i * E : (i + 1) * E] for i in range(N_X * LINES)]
-    positive = jnp.zeros((8, E), jnp.float32)
-    for piece in range(N_X):
-        match = match_ref[piece * R : (piece + 1) * R] * queries_ref[piece, 0:R].astype(jnp.float32)
-        positive = positive + jnp.sum(match.reshape(R // 8, 8, E), axis=0)
-    positive = jnp.sum(positive, axis=(0, 1), keepdims=True)
-    lines = jnp.concatenate(lines + [jnp.broadcast_to(positive, (16 - SLOT, E))], axis=0)
+    lines = jnp.concatenate(lines + [positive_ref[0 : 16 - SLOT]], axis=0)
     for i in range(N_BLOCK):
         line_ref[i] = lines
 
@@ -173,11 +170,15 @@
 
 
 def direction_kernel(
-    plan_ref, own_ref, others_ref, keys_ref, far_ref, match_ref, mine_ref, sums_ref, out_ref, held, both
+    plan_ref, own_ref, others_ref, keys_ref, far_ref, match_ref, mine_ref, sums_ref, out_ref, loss_ref, held, both
 ):
     zl, y, c = (lax.axis_index(a) for a in BLOCK)
     here = (zl * 4 + y) * 2 + c
     held[...] = sums_ref[...].astype(jnp.float32)
+    loss = held[0, LOSS : LOSS + 3, :]
+    for i in range(1, N_ZH * N_ZL):
+        loss = loss + held[i, LOSS : LOSS + 3, :]
+    loss_ref[...] = jnp.sum(loss, axis=0, keepdims=True)[:, 0:1] / (N_BLOCK * BLOCK_ROWS)
     for t in range(ROUNDS + 1):
         other = here if t == 0 else plan_ref[t - 1, here]
         level = other // NEAR
@@ -238,22 +239,25 @@
 def body(embed, partner, plan):
     far = ROUNDS * GATHERED
     with jax.named_scope("normalize"):
-        rounded, sent = call(
-            normalize_kernel, (bf16(R, E), bf16(N_X, SENT, E)), embed, partner.reshape(LINES, E)
-        )
-    with jax.named_scope("queries"):
-        queries = exchange(sent, "x")
+        rounded, sent = pl.pallas_call(
+            normalize_kernel,
+            grid=(1,),
+            out_shape=(bf16(R, E), bf16(SENT, E)),
+            in_specs=[pl.BlockSpec((R, E), lambda g: (0, 0)), pl.BlockSpec((LINES, E), lambda g: (0, 0))],
+            out_specs=(whole, whole),
+        )(embed, partner.reshape(LINES, E))
     with jax.named_scope("own"):
         keys = lax.all_gather(rounded, "zh", axis=0, tiled=True)
     with jax.named_scope("opponents"):
         chunks = exchange(keys.reshape(N_BLOCK, CHUNK, E), BLOCK)
-        chosen = call(select_kernel, bf16(N_BLOCK, ROUNDS, CHUNK, E), plan, chunks, queries,
-            specs=[smem, whole, anywhere])
+        chosen = call(select_kernel, bf16(N_BLOCK, ROUNDS, CHUNK, E), plan, chunks, specs=[smem, whole])
         others = exchange(chosen, BLOCK)
+    with jax.named_scope("queries"):
+        queries = lax.all_gather(sent, "x", axis=0)
     with jax.named_scope("own"):
-        own_exps, match, total = call(
+        own_exps, match, total, positive = call(
             own_kernel,
-            (bf16(N_X * R, GATHERED), f32(N_X * R, E), f32(N_X * R, E)),
+            (bf16(N_X * R, GATHERED), f32(N_X * R, E), f32(N_X * R, E), f32(8, E)),
             queries,
             keys,
             cost_estimate=cost(GATHERED),
@@ -264,7 +268,7 @@
             (bf16(N_X * R, far), f32(N_BLOCK, 16, E)),
             queries,
             others,
-            match,
+            positive,
             total,
             scratch_shapes=[pltpu.VMEM((N_X * R, E), jnp.float32)],
             cost_estimate=cost(far),
@@ -278,11 +282,10 @@
             scratch_shapes=[pltpu.VMEM((NEAR, 2, 16, E), jnp.float32)],
         )
         level = exchange(level, COLUMN)
-        loss = jnp.sum(level[:, LOSS : LOSS + 3, 0].astype(jnp.float32)) / (N_BLOCK * BLOCK_ROWS)
     with jax.named_scope("direction"):
-        parts = call(
+        parts, loss = call(
             direction_kernel,
-            f32(N_X, R, E),
+            (f32(N_X, R, E), f32(1, 1)),
             plan,
             own_exps,
             exps,
@@ -301,7 +304,7 @@
         parts = exchange(parts, "x")
     with jax.named_scope("finish"):
         grad = call(finish_kernel, f32(R, E), embed, parts)
-    return (grad, log_partition.reshape(R), loss)
+    return (grad, log_partition.reshape(R), loss.reshape(()))
 
 
 def solution(mesh):

time: 150 us -> 142 us (0.947)
  blocking collectives: 85.9 us -> 114 us
  waiting for transfers between devices: 25.5 us -> 1.5 us
  starting transfers between devices: 12.8 us -> 5.02 us
  between operations: 2.48 us -> 0.69 us
  local copies, waits for them, and re-layouts: 4.42 us -> 2.81 us
    all_to_all x3 -> x1, waiting for transfers between devices: 25.5 us -> 1.5 us  [exchange(): return lax.all_to_all(value, axes, 0, 0, tiled=True)]
    all_to_all x3 -> x4, blocking collectives: 57 us -> 71.1 us  [exchange(): return lax.all_to_all(value, axes, 0, 0, tiled=True)]
    all_gather x0 -> x1, blocking collectives: none -> 13.1 us  [body(): queries = lax.all_gather(sent, 'x', axis=0)]
    all_to_all x3 -> x1, starting transfers between devices: 12.8 us -> 5.02 us  [exchange(): return lax.all_to_all(value, axes, 0, 0, tiled=True)]
    pallas_call x0 -> x1, Pallas kernels: none -> 1.74 us  [body(): pl.pallas_call(normalize_kernel, grid=(1,), out_shape=(bf16(R, E), bf16(S...]
    unnamed x16 -> x12, local copies, waits for them, and re-layouts: 4.42 us -> 2.81 us
    pallas_call x7 -> x6, Pallas kernels: 17.2 us -> 16 us  [call(): pl.pallas_call(kernel, out_shape=out_shape, in_specs=specs or [whole] * l...]
  transfers between devices with their start and end apart: 3 -> 1, of which waited for: 2 -> 1; matrix products, arithmetic and copies ran while one was open for 0% -> 0% of each run, Pallas kernels for 2% -> 3%
where the time goes in v4:
time: 142 us; the launch traced here: 141 us
  blocking collectives  114 us (80%)
  Pallas kernels  17.7 us (12%)
  starting transfers between devices  5.02 us (4%)
  local copies, waits for them, and re-layouts  2.81 us (2%)
  waiting for transfers between devices  1.5 us (1%)
    all_to_all x4, blocking collectives, exchange(): return lax.all_to_all(value, axes, 0, 0, tiled=True)  71.1 us
    all_gather x1, blocking collectives, body(): keys = lax.all_gather(rounded, 'zh', axis=0, tiled=True)  29.6 us
    pallas_call x6, Pallas kernels, call(): pl.pallas_call(kernel, out_shape=out_shape, in_specs=specs or [whole] * l...  16 us
    all_gather x1, blocking collectives, body(): queries = lax.all_gather(sent, 'x', axis=0)  13.1 us
    all_to_all x1, starting transfers between devices, exchange(): return lax.all_to_all(value, axes, 0, 0, tiled=True)  5.02 us
  transfers between devices with their start and end apart: 1, of which 1 were waited for; matrix products, arithmetic and copies ran while one was open for 0% of the time, Pallas kernels for 3%

profile of v4, /device:TPU:32, one launch (start us, length us, event | category | flops | bytes accessed | tf_op | source)
XLA Modules:
  0.0 141.5 jit_solution(3070258131048300610)
XLA Ops:
  0.6 1.7 %normalize.1 = (bf16[384,128]{1,0:T(8,128)(2,1)}, bf16[400,128]{1,0:T(8,128)(2,1)}) custom-call(f32[384,128]{1,0:T(8,128)} %embed_ref.3, s32[3,128]{1,0:T(4,128)} %bitcast.10), custom_call_target="tpu_custom_call" | custom-call | tf_op jit(solution)/shard_map/normalize/pallas_call | solution.py:242
  2.4 0.0 copy-start.3
  2.4 29.6 %all_gather.11.keys_ref = bf16[1536,128]{1,0:T(8,128)(2,1)S(1)} all-gather(bf16[384,128]{1,0:T(8,128)(2,1)} %get-tuple-element.17), channel_id=1, replica_groups=mesh['zl'=4,'y'=4,'c'=2,'x'=4,'zh'=4] {'zh'}, dimensions={0}, use_global_device_ids=true | all-gather | bytes 491520 | tf_op jit(solution)/shard_map/own/all_gather | solution.py:250
  31.9 19.7 %all_to_all.25.chunks_ref = bf16[32,48,128]{2,1,0:T(8,128)(2,1)S(1)} all-to-all(bf16[32,48,128]{2,1,0:T(8,128)(2,1)S(1)} %bitcast.7), channel_id=1, replica_groups=mesh['zl'=4,'y'=4,'c'=2,'x'=4,'zh'=4] {'zl','y','c'}, dimensions={0} | all-to-all | bytes 786432 | tf_op jit(solution)/shard_map/opponents/all_to_all | solution.py:220
  51.6 0.7 copy-done.2
  52.3 1.5 %opponents.1 = bf16[32,2,48,128]{3,2,1,0:T(8,128)(2,1)} custom-call(s32[2,32]{1,0:T(2,128)S(1)} %copy-done.2, bf16[32,48,128]{2,1,0:T(8,128)(2,1)S(1)} %all_to_all.25.chunks_ref), custom_call_target="tpu_custom_call" | custom-call | tf_op jit(solution)/shard_map/opponents/pallas_call | solution.py:224
  53.8 5.0 %all-to-all-start.1 = ((bf16[32,2,48,128]{3,2,1,0:T(8,128)(2,1)}), bf16[32,2,48,128]{3,2,1,0:T(8,128)(2,1)S(1)}, u32[]{:S(2)}, u32[]{:S(2)}) async-start(bf16[32,2,48,128]{3,2,1,0:T(8,128)(2,1)} %opponents.1), calls=%async_computation.1 | async-start | bytes 1572864 | tf_op jit(solution)/shard_map/opponents/all_to_all | solution.py:220
  58.8 13.1 %all-gather = bf16[1600,128]{1,0:T(8,128)(2,1)S(1)} all-gather(bf16[400,128]{1,0:T(8,128)(2,1)} %get-tuple-element.16), channel_id=2, replica_groups=mesh['zl'=4,'y'=4,'c'=2,'x'=4,'zh'=4] {'x'}, dimensions={0}, use_global_device_ids=true | all-gather | bytes 512000 | tf_op jit(solution)/shard_map/queries/all_gather | solution.py:256
  72.0 3.7 %own.1 = (bf16[1536,1536]{1,0:T(8,128)(2,1)S(1)}, f32[1536,128]{1,0:T(8,128)S(1)}, f32[1536,128]{1,0:T(8,128)S(1)}, f32[8,128]{1,0:T(8,128)S(1)}) custom-call(bf16[4,400,128]{2,1,0:T(8,128)(2,1)S(1)} %bitcast.8, bf16[1536,128]{1,0:T(8,128)(2,1)S(1)} %all_gather.11.keys_ref), custom_call_target="tpu_custom_call" | custom-call | flops 603979776 | bytes 4718592 | tf_op jit(solution)/shard_map/own/pallas_call | solution.py:224
  75.7 0.0 copy-start
  75.7 2.1 %copy-done = bf16[1536,1536]{1,0:T(8,128)(2,1)} copy-done((bf16[1536,1536]{1,0:T(8,128)(2,1)}, bf16[1536,1536]{1,0:T(8,128)(2,1)S(1)}, u32[]{:S(2)}) %copy-start) | copy-done | bytes 4718616
  77.8 1.5 %all-to-all-done.1.keys_ref.far_ref = bf16[32,2,48,128]{3,2,1,0:T(8,128)(2,1)S(1)} async-done(((bf16[32,2,48,128]{3,2,1,0:T(8,128)(2,1)}), bf16[32,2,48,128]{3,2,1,0:T(8,128)(2,1)S(1)}, u32[]{:S(2)}, u32[]{:S(2)}) %all-to-all-start.1) | async-done | bytes 786464 | tf_op jit(solution)/shard_map/opponents/all_to_all | solution.py:220
  79.3 4.2 %others.1 = (bf16[1536,3072]{1,0:T(8,128)(2,1)S(1)}, f32[32,16,128]{2,1,0:T(8,128)S(1)}) custom-call(bf16[4,400,128]{2,1,0:T(8,128)(2,1)S(1)} %bitcast.9, bf16[32,2,48,128]{3,2,1,0:T(8,128)(2,1)S(1)} %all-to-all-done.1.keys_ref.far_ref, f32[8,128]{1,0:T(8,128)S(1)} %get-tuple-element.19.positive_ref, f32[1536,128]{1,0:T(8,128)S(1)} %get-tuple-element.20.own_ref), custom_call_target="tpu_custom_call" | custom-call | flops 1207959552 | bytes 9437184 | tf_op jit(solution)/shard_map/others/pallas_call | solution.py:224
  83.5 0.0 copy-start.1
  83.5 14.5 %all_to_all.26.line_ref = f32[32,16,128]{2,1,0:T(8,128)S(1)} all-to-all(f32[32,16,128]{2,1,0:T(8,128)S(1)} %get-tuple-element.23), channel_id=1, replica_groups=mesh['zl'=4,'y'=4,'c'=2,'x'=4,'zh'=4] {'y','x','c'}, dimensions={0} | all-to-all | bytes 524288 | tf_op jit(solution)/shard_map/sums/all_to_all | solution.py:220
  98.0 0.6 sums.1
  98.6 22.4 %all_to_all.27.sums_ref = bf16[16,32,128]{2,1,0:T(8,128)(2,1)S(1)} all-to-all(bf16[16,32,128]{2,1,0:T(8,128)(2,1)S(1)} %get-tuple-element.25), channel_id=1, replica_groups=mesh['zl'=4,'y'=4,'c'=2,'x'=4,'zh'=4] {'zh','zl'}, dimensions={0} | all-to-all | bytes 262144 | tf_op jit(solution)/shard_map/sums/all_to_all | solution.py:220
  121.0 0.0 copy-done.3
  121.0 0.0 slice-done
  121.1 0.0 slice-done.1
  121.1 5.1 %direction.1 = (f32[4,384,128]{2,1,0:T(8,128)S(1)}, f32[1,1]{1,0:T(1,128)}) custom-call(s32[2,32]{1,0:T(2,128)S(1)} %copy-done.3, bf16[1536,1536]{1,0:T(8,128)(2,1)S(1)} %bitcast.6, bf16[1536,3072]{1,0:T(8,128)(2,1)S(1)} %get-tuple-element.21.others_ref, bf16[1536,128]{1,0:T(8,128)(2,1)S(1)} %all_gather.11.keys_ref, ...), custom_call_target="tpu_custom_call" | custom-call | flops 1811939328 | bytes 14155776 | tf_op jit(solution)/shard_map/direction/pallas_call | solution.py:224
  126.1 14.4 %all_to_all.28.parts_ref = f32[4,384,128]{2,1,0:T(8,128)S(1)} all-to-all(f32[4,384,128]{2,1,0:T(8,128)S(1)} %get-tuple-element.26), channel_id=1, replica_groups=mesh['zl'=4,'y'=4,'c'=2,'x'=4,'zh'=4] {'x'}, dimensions={0} | all-to-all | bytes 1572864 | tf_op jit(solution)/shard_map/direction/all_to_all | solution.py:220
  140.6 0.0 copy-done.1
  140.6 0.9 finish.1
  (4 shorter events, 0.0 us)
Async XLA Ops:
  2.4 118.7 %copy-start.3 = (s32[2,32]{1,0:T(2,128)S(1)}, s32[2,32]{1,0:T(2,128)}, u32[]{:S(2)}) copy-start(s32[2,32]{1,0:T(2,128)} %plan_ref.3) | copy-start | bytes 772
  51.6 0.7 copy-start.2
  53.8 25.5 %all-to-all-start.1 = ((bf16[32,2,48,128]{3,2,1,0:T(8,128)(2,1)}), bf16[32,2,48,128]{3,2,1,0:T(8,128)(2,1)S(1)}, u32[]{:S(2)}, u32[]{:S(2)}) async-start(bf16[32,2,48,128]{3,2,1,0:T(8,128)(2,1)} %opponents.1), calls=%async_computation.1 | async-start | bytes 1572864 | tf_op jit(solution)/shard_map/opponents/all_to_all | solution.py:220
  75.7 2.1 %copy-start = (bf16[1536,1536]{1,0:T(8,128)(2,1)}, bf16[1536,1536]{1,0:T(8,128)(2,1)S(1)}, u32[]{:S(2)}) copy-start(bf16[1536,1536]{1,0:T(8,128)(2,1)S(1)} %get-tuple-element.18.own_ref) | copy-start | bytes 14155780
  79.3 41.8 %slice-start = ((s8[4718592]{0:T(1024)(128)(4,1)}), s8[4194304]{0:T(1024)(128)(4,1)S(1)}, s32[]{:S(2)}) async-start(s8[4718592]{0:T(1024)(128)(4,1)} %bitcast.5), calls=%async_computation.5 | async-start | bytes 8388608
  79.3 41.8 %slice-start.1 = ((s8[4718592]{0:T(1024)(128)(4,1)}), s8[524288]{0:T(1024)(128)(4,1)S(1)}, s32[]{:S(2)}) async-start(s8[4718592]{0:T(1024)(128)(4,1)} %bitcast.5), calls=%async_computation.6 | async-start | bytes 1048576
  83.5 57.1 %copy-start.1 = (f32[384,128]{1,0:T(8,128)S(1)}, f32[384,128]{1,0:T(8,128)}, u32[]{:S(2)}) copy-start(f32[384,128]{1,0:T(8,128)} %embed_ref.3) | copy-start | bytes 589828

commit v5 on v4

--- a/solution.py
+++ b/solution.py
@@ -14,8 +14,8 @@
 AXES = ("zl", "y", "c", "x", "zh")
 SIZES = (4, 4, 2, 4, 4)
 BLOCK = ("zl", "y", "c")
-PLANE = ("y", "x", "c")
-COLUMN = ("zh", "zl")
+PLANE = ("c", "y", "x")
+COLUMN = ("zl", "zh")
 
 R = 384
 E = 128
@@ -88,9 +88,12 @@
 
 
 def select_kernel(plan_ref, chunks_ref, out_ref):
-    for b in range(N_BLOCK):
-        for t in range(ROUNDS):
-            out_ref[b, t] = chunks_ref[plan_ref[t, b]]
+    for start in range(0, N_BLOCK, 8):
+        several = range(start, start + 8)
+        taken = [[chunks_ref[plan_ref[t, b]] for t in range(ROUNDS)] for b in several]
+        for b in several:
+            for t in range(ROUNDS):
+                out_ref[b, t] = taken[b - start][t]
 
 
 def own_kernel(queries_ref, keys_ref, exp_ref, match_ref, total_ref, positive_ref):
@@ -107,7 +110,7 @@
         partner = widen(to_column(index)).astype(jnp.int32) - x * GATHERED - lane
         for z in range(N_ZH):
             k = keys_ref[z * R : (z + 1) * R]
-            e = jnp.exp2(scores(q, k) * SCALE - SCALE)
+            e = jnp.exp2(scores(q, k) * SCALE)
             e = jnp.where(itself == (x - piece) * GATHERED + (z - zh) * R, 0.0, e)
             exp_ref[rows, z * R : (z + 1) * R] = e.astype(jnp.bfloat16)
             chosen = jnp.where(partner == z * R, 1.0, 0.0).astype(jnp.bfloat16)
@@ -130,7 +133,7 @@
             at = (t * N_ZH + z) * R
             for piece in range(N_X):
                 rows = slice(piece * R, (piece + 1) * R)
-                e = jnp.exp2(scores(queries_ref[piece, 0:R], k) * SCALE - SCALE)
+                e = jnp.exp2(scores(queries_ref[piece, 0:R], k) * SCALE)
                 exp_ref[rows, at : at + R] = e.astype(jnp.bfloat16)
                 total[rows] = fold(e) + (total[rows] if at > 0 else own_ref[rows])
     sums = lane_sums(total[...])
@@ -147,11 +150,12 @@
     loss = jnp.zeros((16, E), jnp.float32)
     for i in range(NEAR):
         y, c = divmod(i, 2)
-        part = line_ref[y * 8 + c]
+        at = (c * 4 + y) * N_X
+        part = line_ref[at]
         for j in range(1, N_X):
-            part = part + line_ref[y * 8 + j * 2 + c]
+            part = part + line_ref[at + j]
         sums = jnp.where(slot < SLOT, part, 1.0)
-        logs = INVERSE_TAU + jnp.log(sums)
+        logs = jnp.log(sums)
         loss = loss + jnp.where(slot < SLOT, logs, 0.0)
         loss = loss - jnp.where(slot == SLOT, part * (INVERSE_TAU / E), 0.0)
         held[i, 0] = 1.0 / sums
@@ -184,7 +188,7 @@
         level = other // NEAR
         near = other - level * NEAR
         for z in range(N_ZH):
-            inverse = to_column(as_row(held[z * N_ZL + level, pl.ds(near * LINES, LINES), :]))
+            inverse = to_column(as_row(held[level * N_ZH + z, pl.ds(near * LINES, LINES), :]))
             k = keys_ref[z * R : (z + 1) * R] if t == 0 else far_keys(far_ref, t - 1, z)
             at = (t * N_ZH + z) * R
             both[at : at + R, 0:E] = k

time: 142 us -> 141 us (level)
  Pallas kernels: 17.7 us -> 16.1 us
    pallas_call x6, Pallas kernels: 16 us -> 14.3 us  [call(): pl.pallas_call(kernel, out_shape=out_shape, in_specs=specs or [whole] * l...]
  transfers between devices with their start and end apart: 1 -> 1, of which waited for: 1 -> 1; matrix products, arithmetic and copies ran while one was open for 0% -> 0% of each run, Pallas kernels for 3% -> 2%
where the time goes in v5:
time: 141 us; the launch traced here: 140 us
  blocking collectives  114 us (81%)
  Pallas kernels  16.1 us (11%)
  starting transfers between devices  5.02 us (4%)
  local copies, waits for them, and re-layouts  2.81 us (2%)
  waiting for transfers between devices  1.8 us (1%)
    all_to_all x4, blocking collectives, exchange(): return lax.all_to_all(value, axes, 0, 0, tiled=True)  71.1 us
    all_gather x1, blocking collectives, body(): keys = lax.all_gather(rounded, 'zh', axis=0, tiled=True)  29.6 us
    pallas_call x6, Pallas kernels, call(): pl.pallas_call(kernel, out_shape=out_shape, in_specs=specs or [whole] * l...  14.3 us
    all_gather x1, blocking collectives, body(): queries = lax.all_gather(sent, 'x', axis=0)  13.1 us
    all_to_all x1, starting transfers between devices, exchange(): return lax.all_to_all(value, axes, 0, 0, tiled=True)  5.02 us
  transfers between devices with their start and end apart: 1, of which 1 were waited for; matrix products, arithmetic and copies ran while one was open for 0% of the time, Pallas kernels for 2%

profile of v5, /device:TPU:32, one launch (start us, length us, event | category | flops | bytes accessed | tf_op | source)
XLA Modules:
  0.0 140.1 jit_solution(11898727542317884350)
XLA Ops:
  0.6 1.7 %normalize.1 = (bf16[384,128]{1,0:T(8,128)(2,1)}, bf16[400,128]{1,0:T(8,128)(2,1)}) custom-call(f32[384,128]{1,0:T(8,128)} %embed_ref.3, s32[3,128]{1,0:T(4,128)} %bitcast.10), custom_call_target="tpu_custom_call" | custom-call | tf_op jit(solution)/shard_map/normalize/pallas_call | solution.py:246
  2.4 0.0 copy-start.3
  2.4 29.6 %all_gather.11.keys_ref = bf16[1536,128]{1,0:T(8,128)(2,1)S(1)} all-gather(bf16[384,128]{1,0:T(8,128)(2,1)} %get-tuple-element.17), channel_id=1, replica_groups=mesh['zl'=4,'y'=4,'c'=2,'x'=4,'zh'=4] {'zh'}, dimensions={0}, use_global_device_ids=true | all-gather | bytes 491520 | tf_op jit(solution)/shard_map/own/all_gather | solution.py:254
  31.9 19.7 %all_to_all.25.chunks_ref = bf16[32,48,128]{2,1,0:T(8,128)(2,1)S(1)} all-to-all(bf16[32,48,128]{2,1,0:T(8,128)(2,1)S(1)} %bitcast.7), channel_id=1, replica_groups=mesh['zl'=4,'y'=4,'c'=2,'x'=4,'zh'=4] {'zl','y','c'}, dimensions={0} | all-to-all | bytes 786432 | tf_op jit(solution)/shard_map/opponents/all_to_all | solution.py:224
  51.6 0.7 copy-done.2
  52.3 1.5 %opponents.1 = bf16[32,2,48,128]{3,2,1,0:T(8,128)(2,1)} custom-call(s32[2,32]{1,0:T(2,128)S(1)} %copy-done.2, bf16[32,48,128]{2,1,0:T(8,128)(2,1)S(1)} %all_to_all.25.chunks_ref), custom_call_target="tpu_custom_call" | custom-call | tf_op jit(solution)/shard_map/opponents/pallas_call | solution.py:228
  53.8 5.0 %all-to-all-start.1 = ((bf16[32,2,48,128]{3,2,1,0:T(8,128)(2,1)}), bf16[32,2,48,128]{3,2,1,0:T(8,128)(2,1)S(1)}, u32[]{:S(2)}, u32[]{:S(2)}) async-start(bf16[32,2,48,128]{3,2,1,0:T(8,128)(2,1)} %opponents.1), calls=%async_computation.1 | async-start | bytes 1572864 | tf_op jit(solution)/shard_map/opponents/all_to_all | solution.py:224
  58.8 13.1 %all-gather = bf16[1600,128]{1,0:T(8,128)(2,1)S(1)} all-gather(bf16[400,128]{1,0:T(8,128)(2,1)} %get-tuple-element.16), channel_id=2, replica_groups=mesh['zl'=4,'y'=4,'c'=2,'x'=4,'zh'=4] {'x'}, dimensions={0}, use_global_device_ids=true | all-gather | bytes 512000 | tf_op jit(solution)/shard_map/queries/all_gather | solution.py:260
  72.0 3.4 %own.1 = (bf16[1536,1536]{1,0:T(8,128)(2,1)S(1)}, f32[1536,128]{1,0:T(8,128)S(1)}, f32[1536,128]{1,0:T(8,128)S(1)}, f32[8,128]{1,0:T(8,128)S(1)}) custom-call(bf16[4,400,128]{2,1,0:T(8,128)(2,1)S(1)} %bitcast.8, bf16[1536,128]{1,0:T(8,128)(2,1)S(1)} %all_gather.11.keys_ref), custom_call_target="tpu_custom_call" | custom-call | flops 603979776 | bytes 4718592 | tf_op jit(solution)/shard_map/own/pallas_call | solution.py:228
  75.4 0.0 copy-start
  75.4 2.1 %copy-done = bf16[1536,1536]{1,0:T(8,128)(2,1)} copy-done((bf16[1536,1536]{1,0:T(8,128)(2,1)}, bf16[1536,1536]{1,0:T(8,128)(2,1)S(1)}, u32[]{:S(2)}) %copy-start) | copy-done | bytes 4718616
  77.5 1.8 %all-to-all-done.1.keys_ref.far_ref = bf16[32,2,48,128]{3,2,1,0:T(8,128)(2,1)S(1)} async-done(((bf16[32,2,48,128]{3,2,1,0:T(8,128)(2,1)}), bf16[32,2,48,128]{3,2,1,0:T(8,128)(2,1)S(1)}, u32[]{:S(2)}, u32[]{:S(2)}) %all-to-all-start.1) | async-done | bytes 786464 | tf_op jit(solution)/shard_map/opponents/all_to_all | solution.py:224
  79.3 2.8 %others.1 = (bf16[1536,3072]{1,0:T(8,128)(2,1)S(1)}, f32[32,16,128]{2,1,0:T(8,128)S(1)}) custom-call(bf16[4,400,128]{2,1,0:T(8,128)(2,1)S(1)} %bitcast.9, bf16[32,2,48,128]{3,2,1,0:T(8,128)(2,1)S(1)} %all-to-all-done.1.keys_ref.far_ref, f32[8,128]{1,0:T(8,128)S(1)} %get-tuple-element.19.positive_ref, f32[1536,128]{1,0:T(8,128)S(1)} %get-tuple-element.20.own_ref), custom_call_target="tpu_custom_call" | custom-call | flops 1207959552 | bytes 9437184 | tf_op jit(solution)/shard_map/others/pallas_call | solution.py:228
  82.1 0.0 copy-start.1
  82.2 14.8 %all_to_all.26.line_ref = f32[32,16,128]{2,1,0:T(8,128)S(1)} all-to-all(f32[32,16,128]{2,1,0:T(8,128)S(1)} %get-tuple-element.23), channel_id=1, replica_groups=mesh['zl'=4,'y'=4,'c'=2,'x'=4,'zh'=4] {'c','y','x'}, dimensions={0} | all-to-all | bytes 524288 | tf_op jit(solution)/shard_map/sums/all_to_all | solution.py:224
  96.9 0.6 sums.1
  97.5 22.7 %all_to_all.27.sums_ref = bf16[16,32,128]{2,1,0:T(8,128)(2,1)S(1)} all-to-all(bf16[16,32,128]{2,1,0:T(8,128)(2,1)S(1)} %get-tuple-element.25), channel_id=1, replica_groups=mesh['zl'=4,'y'=4,'c'=2,'x'=4,'zh'=4] {'zl','zh'}, dimensions={0} | all-to-all | bytes 262144 | tf_op jit(solution)/shard_map/sums/all_to_all | solution.py:224
  120.3 0.0 copy-done.3
  120.3 0.0 slice-done
  120.3 0.0 slice-done.1
  120.3 5.1 %direction.1 = (f32[4,384,128]{2,1,0:T(8,128)S(1)}, f32[1,1]{1,0:T(1,128)}) custom-call(s32[2,32]{1,0:T(2,128)S(1)} %copy-done.3, bf16[1536,1536]{1,0:T(8,128)(2,1)S(1)} %bitcast.6, bf16[1536,3072]{1,0:T(8,128)(2,1)S(1)} %get-tuple-element.21.others_ref, bf16[1536,128]{1,0:T(8,128)(2,1)S(1)} %all_gather.11.keys_ref, ...), custom_call_target="tpu_custom_call" | custom-call | flops 1811939328 | bytes 14155776 | tf_op jit(solution)/shard_map/direction/pallas_call | solution.py:228
  125.4 13.9 %all_to_all.28.parts_ref = f32[4,384,128]{2,1,0:T(8,128)S(1)} all-to-all(f32[4,384,128]{2,1,0:T(8,128)S(1)} %get-tuple-element.26), channel_id=1, replica_groups=mesh['zl'=4,'y'=4,'c'=2,'x'=4,'zh'=4] {'x'}, dimensions={0} | all-to-all | bytes 1572864 | tf_op jit(solution)/shard_map/direction/all_to_all | solution.py:224
  139.2 0.0 copy-done.1
  139.2 0.9 finish.1
  (4 shorter events, 0.0 us)
Async XLA Ops:
  2.4 117.9 %copy-start.3 = (s32[2,32]{1,0:T(2,128)S(1)}, s32[2,32]{1,0:T(2,128)}, u32[]{:S(2)}) copy-start(s32[2,32]{1,0:T(2,128)} %plan_ref.3) | copy-start | bytes 772
  51.6 0.7 copy-start.2
  53.8 25.5 %all-to-all-start.1 = ((bf16[32,2,48,128]{3,2,1,0:T(8,128)(2,1)}), bf16[32,2,48,128]{3,2,1,0:T(8,128)(2,1)S(1)}, u32[]{:S(2)}, u32[]{:S(2)}) async-start(bf16[32,2,48,128]{3,2,1,0:T(8,128)(2,1)} %opponents.1), calls=%async_computation.1 | async-start | bytes 1572864 | tf_op jit(solution)/shard_map/opponents/all_to_all | solution.py:224
  75.4 2.1 %copy-start = (bf16[1536,1536]{1,0:T(8,128)(2,1)}, bf16[1536,1536]{1,0:T(8,128)(2,1)S(1)}, u32[]{:S(2)}) copy-start(bf16[1536,1536]{1,0:T(8,128)(2,1)S(1)} %get-tuple-element.18.own_ref) | copy-start | bytes 14155780
  79.3 41.0 %slice-start = ((s8[4718592]{0:T(1024)(128)(4,1)}), s8[4194304]{0:T(1024)(128)(4,1)S(1)}, s32[]{:S(2)}) async-start(s8[4718592]{0:T(1024)(128)(4,1)} %bitcast.5), calls=%async_computation.5 | async-start | bytes 8388608
  79.3 41.0 %slice-start.1 = ((s8[4718592]{0:T(1024)(128)(4,1)}), s8[524288]{0:T(1024)(128)(4,1)S(1)}, s32[]{:S(2)}) async-start(s8[4718592]{0:T(1024)(128)(4,1)} %bitcast.5), calls=%async_computation.6 | async-start | bytes 1048576
  82.1 57.1 %copy-start.1 = (f32[384,128]{1,0:T(8,128)S(1)}, f32[384,128]{1,0:T(8,128)}, u32[]{:S(2)}) copy-start(f32[384,128]{1,0:T(8,128)} %embed_ref.3) | copy-start | bytes 589828

commit v6 on v5

--- a/solution.py
+++ b/solution.py
@@ -11,11 +11,12 @@
 INVERSE_TAU = 10.0
 SCALE = INVERSE_TAU * float(np.log2(np.e))
 
-AXES = ("zl", "y", "c", "x", "zh")
-SIZES = (4, 4, 2, 4, 4)
-BLOCK = ("zl", "y", "c")
+AXES = ("zu", "zl", "y", "c", "x", "zh")
+SIZES = (2, 2, 4, 2, 4, 4)
+BLOCK = ("zu", "zl", "y", "c")
+HALF = ("zl", "y", "c")
 PLANE = ("c", "y", "x")
-COLUMN = ("zl", "zh")
+COLUMN = ("zu", "zl", "zh")
 
 R = 384
 E = 128
@@ -25,16 +26,18 @@
 N_ZH = 4
 GATHERED = R * N_ZH
 BLOCK_ROWS = GATHERED * N_X
-CHUNK = GATHERED // N_BLOCK
+N_HALF = N_BLOCK // 2
+CHUNK = GATHERED // N_HALF
 SENT = R + 16
 LINES = R // E
 SLOT = LINES * N_X
 NEAR = 8
 LOSS = LINES * NEAR
-VMEM = 12 * 1024 * 1024
+VMEM = 5 * 1024 * 1024
 
 whole = pl.BlockSpec(memory_space=pltpu.VMEM)
 smem = pl.BlockSpec(memory_space=pltpu.SMEM)
+anywhere = pl.BlockSpec(memory_space=pl.ANY)
 
 
 def as_row(lines):
@@ -73,7 +76,7 @@
     return jnp.concatenate([keys_ref[z * each + i, t] for i in range(each)], axis=0)
 
 
-def normalize_kernel(embed_ref, partner_ref, rounded_ref, sent_ref):
+def normalize_kernel(embed_ref, partner_ref, plan_ref, rounded_ref, sent_ref, copy_ref):
     x = embed_ref[...]
     inverse = lax.rsqrt(jnp.sum(x * x, axis=1, keepdims=True) + 1e-06)
     rounded = (x * inverse).astype(jnp.bfloat16)
@@ -85,48 +88,51 @@
     index = both.astype(jnp.float32).astype(jnp.bfloat16)
     sent_ref[0:R] = rounded
     sent_ref[R:SENT] = index
-
-
-def select_kernel(plan_ref, chunks_ref, out_ref):
-    for start in range(0, N_BLOCK, 8):
-        several = range(start, start + 8)
-        taken = [[chunks_ref[plan_ref[t, b]] for t in range(ROUNDS)] for b in several]
+    copy_ref[...] = plan_ref[...]
+
+
+def select_kernel(plan_ref, chunks_ref, queries_ref, out_ref):
+    first = lax.axis_index("zu") * N_HALF
+    for start in range(0, N_HALF, 4):
+        several = range(start, start + 4)
+        taken = [[chunks_ref[plan_ref[t, first + b]] for t in range(ROUNDS)] for b in several]
         for b in several:
             for t in range(ROUNDS):
                 out_ref[b, t] = taken[b - start][t]
 
 
-def own_kernel(queries_ref, keys_ref, exp_ref, match_ref, total_ref, positive_ref):
+def own_kernel(queries_ref, keys_ref, exp_ref, match_ref, sums_ref):
     x = lax.axis_index("x")
     zh = lax.axis_index("zh")
     lane = lax.broadcasted_iota(jnp.int32, (R, R), 1)
     itself = lax.broadcasted_iota(jnp.int32, (R, R), 0) - lane
     positive = jnp.zeros((8, E), jnp.float32)
+    lines = []
     for piece in range(N_X):
         q = queries_ref[piece, 0:R]
         rows = slice(piece * R, (piece + 1) * R)
         index = queries_ref[piece, R:SENT].astype(jnp.float32)
         index = as_row(index[0:LINES]) * 128.0 + as_row(index[LINES : 2 * LINES])
         partner = widen(to_column(index)).astype(jnp.int32) - x * GATHERED - lane
+        total = jnp.zeros((R, E), jnp.float32)
+        match = jnp.zeros((R, E), jnp.float32)
         for z in range(N_ZH):
             k = keys_ref[z * R : (z + 1) * R]
             e = jnp.exp2(scores(q, k) * SCALE)
             e = jnp.where(itself == (x - piece) * GATHERED + (z - zh) * R, 0.0, e)
             exp_ref[rows, z * R : (z + 1) * R] = e.astype(jnp.bfloat16)
             chosen = jnp.where(partner == z * R, 1.0, 0.0).astype(jnp.bfloat16)
-            match = jnp.dot(chosen, k, preferred_element_type=jnp.float32)
-            part = fold(e)
-            if z > 0:
-                match = match + match_ref[rows]
-                part = part + total_ref[rows]
-            match_ref[rows] = match
-            total_ref[rows] = part
+            match = match + jnp.dot(chosen, k, preferred_element_type=jnp.float32)
+            total = total + fold(e)
+        match_ref[rows] = match.astype(jnp.bfloat16)
+        lines.append(as_lines(lane_sums(total)))
         match = match * q.astype(jnp.float32)
         positive = positive + jnp.sum(match.reshape(R // 8, 8, E), axis=0)
-    positive_ref[...] = jnp.broadcast_to(jnp.sum(positive, axis=(0, 1), keepdims=True), (8, E))
-
-
-def others_kernel(queries_ref, keys_ref, positive_ref, own_ref, exp_ref, line_ref, total):
+    positive = jnp.broadcast_to(jnp.sum(positive, axis=(0, 1), keepdims=True), (16 - SLOT, E))
+    sums_ref[...] = jnp.concatenate(lines + [positive], axis=0)
+
+
+def others_kernel(queries_ref, keys_ref, own_ref, exp_ref, line_ref, total):
     for t in range(ROUNDS):
         for z in range(N_ZH):
             k = far_keys(keys_ref, t, z)
@@ -135,10 +141,10 @@
                 rows = slice(piece * R, (piece + 1) * R)
                 e = jnp.exp2(scores(queries_ref[piece, 0:R], k) * SCALE)
                 exp_ref[rows, at : at + R] = e.astype(jnp.bfloat16)
-                total[rows] = fold(e) + (total[rows] if at > 0 else own_ref[rows])
+                total[rows] = fold(e) + total[rows] if at > 0 else fold(e)
     sums = lane_sums(total[...])
     lines = [sums[0:1, i * E : (i + 1) * E] for i in range(N_X * LINES)]
-    lines = jnp.concatenate(lines + [positive_ref[0 : 16 - SLOT]], axis=0)
+    lines = jnp.concatenate(lines + [jnp.zeros((16 - SLOT, E), jnp.float32)], axis=0) + own_ref[...]
     for i in range(N_BLOCK):
         line_ref[i] = lines
 
@@ -176,8 +182,8 @@
 def direction_kernel(
     plan_ref, own_ref, others_ref, keys_ref, far_ref, match_ref, mine_ref, sums_ref, out_ref, loss_ref, held, both
 ):
-    zl, y, c = (lax.axis_index(a) for a in BLOCK)
-    here = (zl * 4 + y) * 2 + c
+    zu, zl, y, c = (lax.axis_index(a) for a in BLOCK)
+    here = ((zu * 2 + zl) * 4 + y) * 2 + c
     held[...] = sums_ref[...].astype(jnp.float32)
     loss = held[0, LOSS : LOSS + 3, :]
     for i in range(1, N_ZH * N_ZL):
@@ -198,7 +204,7 @@
         total = jnp.dot(own_ref[rows], both[0:GATHERED], preferred_element_type=jnp.float32)
         total = total + jnp.dot(others_ref[rows], both[GATHERED:], preferred_element_type=jnp.float32)
         column = to_column(as_row(mine_ref[piece * LINES : (piece + 1) * LINES, :]))
-        out_ref[piece] = column * total[:, 0:E] + total[:, E : 2 * E] - 2.0 * match_ref[rows]
+        out_ref[piece] = column * total[:, 0:E] + total[:, E : 2 * E] - 2.0 * match_ref[rows].astype(jnp.float32)
 
 
 def finish_kernel(embed_ref, parts_ref, out_ref):
@@ -243,25 +249,27 @@
 def body(embed, partner, plan):
     far = ROUNDS * GATHERED
     with jax.named_scope("normalize"):
-        rounded, sent = pl.pallas_call(
+        given = (embed, partner.reshape(LINES, E), plan)
+        rounded, sent, plan = pl.pallas_call(
             normalize_kernel,
             grid=(1,),
-            out_shape=(bf16(R, E), bf16(SENT, E)),
-            in_specs=[pl.BlockSpec((R, E), lambda g: (0, 0)), pl.BlockSpec((LINES, E), lambda g: (0, 0))],
-            out_specs=(whole, whole),
-        )(embed, partner.reshape(LINES, E))
+            out_shape=(bf16(R, E), bf16(SENT, E), jax.ShapeDtypeStruct(plan.shape, plan.dtype)),
+            in_specs=[pl.BlockSpec(array.shape, lambda g: (0, 0)) for array in given],
+            out_specs=(whole, whole, whole),
+        )(*given)
     with jax.named_scope("own"):
         keys = lax.all_gather(rounded, "zh", axis=0, tiled=True)
-    with jax.named_scope("opponents"):
-        chunks = exchange(keys.reshape(N_BLOCK, CHUNK, E), BLOCK)
-        chosen = call(select_kernel, bf16(N_BLOCK, ROUNDS, CHUNK, E), plan, chunks, specs=[smem, whole])
-        others = exchange(chosen, BLOCK)
     with jax.named_scope("queries"):
         queries = lax.all_gather(sent, "x", axis=0)
+    with jax.named_scope("opponents"):
+        chunks = keys.reshape(N_HALF, CHUNK, E)
+        chunks = exchange(jnp.concatenate([chunks, chunks]), BLOCK)
+        chosen = call(select_kernel, bf16(N_HALF, ROUNDS, CHUNK, E), plan, chunks, queries, specs=[smem, whole, anywhere])
+        others = exchange(chosen, HALF)
     with jax.named_scope("own"):
-        own_exps, match, total, positive = call(
+        own_exps, match, own_sums = call(
             own_kernel,
-            (bf16(N_X * R, GATHERED), f32(N_X * R, E), f32(N_X * R, E), f32(8, E)),
+            (bf16(N_X * R, GATHERED), bf16(N_X * R, E), f32(16, E)),
             queries,
             keys,
             cost_estimate=cost(GATHERED),
@@ -272,8 +280,7 @@
             (bf16(N_X * R, far), f32(N_BLOCK, 16, E)),
             queries,
             others,
-            positive,
-            total,
+            own_sums,
             scratch_shapes=[pltpu.VMEM((N_X * R, E), jnp.float32)],
             cost_estimate=cost(far),
         )

time: 141 us -> 140 us (level)
  blocking collectives: 114 us -> 93 us
  waiting for transfers between devices: 1.8 us -> 13.8 us
  starting transfers between devices: 5.02 us -> 11.9 us
    all_to_all x4 -> x3, blocking collectives: 71.1 us -> 50.5 us  [exchange(): return lax.all_to_all(value, axes, 0, 0, tiled=True)]
    all_to_all x1 -> x2, waiting for transfers between devices: 1.8 us -> 13.8 us  [exchange(): return lax.all_to_all(value, axes, 0, 0, tiled=True)]
    all_to_all x1 -> x2, starting transfers between devices: 5.02 us -> 11.9 us  [exchange(): return lax.all_to_all(value, axes, 0, 0, tiled=True)]
  transfers between devices with their start and end apart: 1 -> 2, of which waited for: 1 -> 2; matrix products, arithmetic and copies ran while one was open for 0% -> 0% of each run, Pallas kernels for 2% -> 3%
where the time goes in v6:
time: 140 us
  blocking collectives  93 us (66%)
  Pallas kernels  16.4 us (12%)
  waiting for transfers between devices  13.8 us (10%)
  starting transfers between devices  11.9 us (8%)
  local copies, waits for them, and re-layouts  2.75 us (2%)
    all_to_all x3, blocking collectives, exchange(): return lax.all_to_all(value, axes, 0, 0, tiled=True)  50.5 us
    all_gather x1, blocking collectives, body(): keys = lax.all_gather(rounded, 'zh', axis=0, tiled=True)  29.4 us
    pallas_call x6, Pallas kernels, call(): pl.pallas_call(kernel, out_shape=out_shape, in_specs=specs or [whole] * l...  14.7 us
    all_to_all x2, waiting for transfers between devices, exchange(): return lax.all_to_all(value, axes, 0, 0, tiled=True)  13.8 us
    all_gather x1, blocking collectives, body(): queries = lax.all_gather(sent, 'x', axis=0)  13.1 us
    all_to_all x2, starting transfers between devices, exchange(): return lax.all_to_all(value, axes, 0, 0, tiled=True)  11.9 us
  transfers between devices with their start and end apart: 2, of which 2 were waited for; matrix products, arithmetic and copies ran while one was open for 0% of the time, Pallas kernels for 3%

profile of v6, /device:TPU:32, one launch (start us, length us, event | category | flops | bytes accessed | tf_op | source)
XLA Modules:
  0.0 139.6 jit_solution(9168301966850220148)
XLA Ops:
  0.6 1.8 %normalize.1 = (bf16[384,128]{1,0:T(8,128)(2,1)}, bf16[400,128]{1,0:T(8,128)(2,1)}, s32[2,32]{1,0:T(2,128)}) custom-call(f32[384,128]{1,0:T(8,128)} %embed_ref.3, s32[3,128]{1,0:T(4,128)} %bitcast.11, s32[2,32]{1,0:T(2,128)} %plan_ref.1), custom_call_target="tpu_custom_call" | custom-call | tf_op jit(solution)/shard_map/normalize/pallas_call | solution.py:253
  2.4 29.4 %all_gather.11.keys_ref = bf16[1536,128]{1,0:T(8,128)(2,1)S(1)} all-gather(bf16[384,128]{1,0:T(8,128)(2,1)} %get-tuple-element.18), channel_id=1, replica_groups=mesh['zu'=2,'zl'=2,'y'=4,'c'=2,'x'=4,'zh'=4] {'zh'}, dimensions={0}, use_global_device_ids=true | all-gather | bytes 491520 | tf_op jit(solution)/shard_map/own/all_gather | solution.py:261
  31.8 1.0 pad_maximum_fusion
  32.8 7.2 %all-to-all-start = ((bf16[32,96,128]{2,1,0:T(8,128)(2,1)}), bf16[32,96,128]{2,1,0:T(8,128)(2,1)S(1)}, u32[]{:S(2)}, u32[]{:S(2)}) async-start(bf16[32,96,128]{2,1,0:T(8,128)(2,1)} %pad_maximum_fusion), calls=%async_computation | async-start | bytes 1572864 | tf_op jit(solution)/shard_map/opponents/all_to_all | solution.py:230
  40.0 0.0 copy-start.3
  40.0 13.1 %all-gather = bf16[1600,128]{1,0:T(8,128)(2,1)S(1)} all-gather(bf16[400,128]{1,0:T(8,128)(2,1)} %get-tuple-element.17), channel_id=2, replica_groups=mesh['zu'=2,'zl'=2,'y'=4,'c'=2,'x'=4,'zh'=4] {'x'}, dimensions={0}, use_global_device_ids=true | all-gather | bytes 512000 | tf_op jit(solution)/shard_map/queries/all_gather | solution.py:263
  53.1 7.3 %all-to-all-done.chunks_ref = bf16[32,96,128]{2,1,0:T(8,128)(2,1)S(1)} async-done(((bf16[32,96,128]{2,1,0:T(8,128)(2,1)}), bf16[32,96,128]{2,1,0:T(8,128)(2,1)S(1)}, u32[]{:S(2)}, u32[]{:S(2)}) %all-to-all-start) | async-done | bytes 786464 | tf_op jit(solution)/shard_map/opponents/all_to_all | solution.py:230
  60.4 0.6 copy-done.2
  61.0 1.5 %opponents.1 = bf16[16,2,96,128]{3,2,1,0:T(8,128)(2,1)} custom-call(s32[2,32]{1,0:T(2,128)S(1)} %copy-done.2, bf16[32,96,128]{2,1,0:T(8,128)(2,1)S(1)} %all-to-all-done.chunks_ref, bf16[4,400,128]{2,1,0:T(8,128)(2,1)S(1)} %bitcast.8), custom_call_target="tpu_custom_call" | custom-call | tf_op jit(solution)/shard_map/opponents/pallas_call | solution.py:234
  62.5 4.7 %all-to-all-start.1 = ((bf16[16,2,96,128]{3,2,1,0:T(8,128)(2,1)}), bf16[16,2,96,128]{3,2,1,0:T(8,128)(2,1)S(1)}, u32[]{:S(2)}, u32[]{:S(2)}) async-start(bf16[16,2,96,128]{3,2,1,0:T(8,128)(2,1)} %opponents.1), calls=%async_computation.1 | async-start | bytes 1572864 | tf_op jit(solution)/shard_map/opponents/all_to_all | solution.py:230
  67.3 3.8 %own.1 = (bf16[1536,1536]{1,0:T(8,128)(2,1)S(1)}, bf16[1536,128]{1,0:T(8,128)(2,1)S(1)}, f32[16,128]{1,0:T(8,128)S(1)}) custom-call(bf16[4,400,128]{2,1,0:T(8,128)(2,1)S(1)} %bitcast.9, bf16[1536,128]{1,0:T(8,128)(2,1)S(1)} %all_gather.11.keys_ref), custom_call_target="tpu_custom_call" | custom-call | flops 603979776 | bytes 4718592 | tf_op jit(solution)/shard_map/own/pallas_call | solution.py:234
  71.0 2.1 %copy-done = bf16[1536,1536]{1,0:T(8,128)(2,1)} copy-done((bf16[1536,1536]{1,0:T(8,128)(2,1)}, bf16[1536,1536]{1,0:T(8,128)(2,1)S(1)}, u32[]{:S(2)}) %copy-start) | copy-done | bytes 4718616
  73.2 6.5 %all-to-all-done.1.keys_ref.far_ref = bf16[16,2,96,128]{3,2,1,0:T(8,128)(2,1)S(1)} async-done(((bf16[16,2,96,128]{3,2,1,0:T(8,128)(2,1)}), bf16[16,2,96,128]{3,2,1,0:T(8,128)(2,1)S(1)}, u32[]{:S(2)}, u32[]{:S(2)}) %all-to-all-start.1) | async-done | bytes 786464 | tf_op jit(solution)/shard_map/opponents/all_to_all | solution.py:230
  79.6 2.8 %others.1 = (bf16[1536,3072]{1,0:T(8,128)(2,1)S(1)}, f32[32,16,128]{2,1,0:T(8,128)S(1)}) custom-call(bf16[4,400,128]{2,1,0:T(8,128)(2,1)S(1)} %bitcast.10, bf16[16,2,96,128]{3,2,1,0:T(8,128)(2,1)S(1)} %all-to-all-done.1.keys_ref.far_ref, f32[16,128]{1,0:T(8,128)S(1)} %get-tuple-element.20.own_ref), custom_call_target="tpu_custom_call" | custom-call | flops 1207959552 | bytes 9437184 | tf_op jit(solution)/shard_map/others/pallas_call | solution.py:234
  82.5 0.0 copy-start.1
  82.5 14.6 %all_to_all.25.line_ref = f32[32,16,128]{2,1,0:T(8,128)S(1)} all-to-all(f32[32,16,128]{2,1,0:T(8,128)S(1)} %get-tuple-element.23), channel_id=1, replica_groups=mesh['zu'=2,'zl'=2,'y'=4,'c'=2,'x'=4,'zh'=4] {'c','y','x'}, dimensions={0} | all-to-all | bytes 524288 | tf_op jit(solution)/shard_map/sums/all_to_all | solution.py:230
  97.1 0.6 sums.1
  97.7 22.0 %all_to_all.26.sums_ref = bf16[16,32,128]{2,1,0:T(8,128)(2,1)S(1)} all-to-all(bf16[16,32,128]{2,1,0:T(8,128)(2,1)S(1)} %get-tuple-element.25), channel_id=1, replica_groups=mesh['zu'=2,'zl'=2,'y'=4,'c'=2,'x'=4,'zh'=4] {'zu','zl','zh'}, dimensions={0} | all-to-all | bytes 262144 | tf_op jit(solution)/shard_map/sums/all_to_all | solution.py:230
  119.7 0.0 copy-done.3
  119.7 0.0 slice-done
  119.7 0.0 slice-done.1
  119.7 5.1 %direction.1 = (f32[4,384,128]{2,1,0:T(8,128)S(1)}, f32[1,1]{1,0:T(1,128)}) custom-call(s32[2,32]{1,0:T(2,128)S(1)} %copy-done.3, bf16[1536,1536]{1,0:T(8,128)(2,1)S(1)} %bitcast.6, bf16[1536,3072]{1,0:T(8,128)(2,1)S(1)} %get-tuple-element.21.others_ref, bf16[1536,128]{1,0:T(8,128)(2,1)S(1)} %all_gather.11.keys_ref, ...), custom_call_target="tpu_custom_call" | custom-call | flops 1811939328 | bytes 14155776 | tf_op jit(solution)/shard_map/direction/pallas_call | solution.py:234
  124.8 13.9 %all_to_all.27.parts_ref = f32[4,384,128]{2,1,0:T(8,128)S(1)} all-to-all(f32[4,384,128]{2,1,0:T(8,128)S(1)} %get-tuple-element.26), channel_id=1, replica_groups=mesh['zu'=2,'zl'=2,'y'=4,'c'=2,'x'=4,'zh'=4] {'x'}, dimensions={0} | all-to-all | bytes 1572864 | tf_op jit(solution)/shard_map/direction/all_to_all | solution.py:230
  138.7 0.9 finish.1
  (6 shorter events, 0.0 us)
Async XLA Ops:
  32.8 27.6 %all-to-all-start = ((bf16[32,96,128]{2,1,0:T(8,128)(2,1)}), bf16[32,96,128]{2,1,0:T(8,128)(2,1)S(1)}, u32[]{:S(2)}, u32[]{:S(2)}) async-start(bf16[32,96,128]{2,1,0:T(8,128)(2,1)} %pad_maximum_fusion), calls=%async_computation | async-start | bytes 1572864 | tf_op jit(solution)/shard_map/opponents/all_to_all | solution.py:230
  40.0 79.7 %copy-start.3 = (s32[2,32]{1,0:T(2,128)S(1)}, s32[2,32]{1,0:T(2,128)}, u32[]{:S(2)}) copy-start(s32[2,32]{1,0:T(2,128)} %get-tuple-element.16.plan_ref) | copy-start | bytes 772
  60.4 0.6 copy-start.2
  62.5 17.1 %all-to-all-start.1 = ((bf16[16,2,96,128]{3,2,1,0:T(8,128)(2,1)}), bf16[16,2,96,128]{3,2,1,0:T(8,128)(2,1)S(1)}, u32[]{:S(2)}, u32[]{:S(2)}) async-start(bf16[16,2,96,128]{3,2,1,0:T(8,128)(2,1)} %opponents.1), calls=%async_computation.1 | async-start | bytes 1572864 | tf_op jit(solution)/shard_map/opponents/all_to_all | solution.py:230
  71.0 2.1 %copy-start = (bf16[1536,1536]{1,0:T(8,128)(2,1)}, bf16[1536,1536]{1,0:T(8,128)(2,1)S(1)}, u32[]{:S(2)}) copy-start(bf16[1536,1536]{1,0:T(8,128)(2,1)S(1)} %get-tuple-element.19.own_ref) | copy-start | bytes 14155780
  79.6 40.1 %slice-start = ((s8[4718592]{0:T(1024)(128)(4,1)}), s8[4194304]{0:T(1024)(128)(4,1)S(1)}, s32[]{:S(2)}) async-start(s8[4718592]{0:T(1024)(128)(4,1)} %bitcast.5), calls=%async_computation.5 | async-start | bytes 8388608
  79.6 40.1 %slice-start.1 = ((s8[4718592]{0:T(1024)(128)(4,1)}), s8[524288]{0:T(1024)(128)(4,1)S(1)}, s32[]{:S(2)}) async-start(s8[4718592]{0:T(1024)(128)(4,1)} %bitcast.5), calls=%async_computation.6 | async-start | bytes 1048576
  82.5 56.2 %copy-start.1 = (f32[384,128]{1,0:T(8,128)S(1)}, f32[384,128]{1,0:T(8,128)}, u32[]{:S(2)}) copy-start(f32[384,128]{1,0:T(8,128)} %embed_ref.3) | copy-start | bytes 589828

commit v7 on v6

--- a/solution.py
+++ b/solution.py
@@ -37,7 +37,6 @@
 
 whole = pl.BlockSpec(memory_space=pltpu.VMEM)
 smem = pl.BlockSpec(memory_space=pltpu.SMEM)
-anywhere = pl.BlockSpec(memory_space=pl.ANY)
 
 
 def as_row(lines):
@@ -91,7 +90,7 @@
     copy_ref[...] = plan_ref[...]
 
 
-def select_kernel(plan_ref, chunks_ref, queries_ref, out_ref):
+def select_kernel(plan_ref, chunks_ref, out_ref):
     first = lax.axis_index("zu") * N_HALF
     for start in range(0, N_HALF, 4):
         several = range(start, start + 4)
@@ -101,7 +100,8 @@
                 out_ref[b, t] = taken[b - start][t]
 
 
-def own_kernel(queries_ref, keys_ref, exp_ref, match_ref, sums_ref):
+def own_kernel(queries_ref, keys_ref, plan_ref, exp_ref, match_ref, sums_ref, copy_ref):
+    copy_ref[...] = plan_ref[...]
     x = lax.axis_index("x")
     zh = lax.axis_index("zh")
     lane = lax.broadcasted_iota(jnp.int32, (R, R), 1)
@@ -261,19 +261,20 @@
         keys = lax.all_gather(rounded, "zh", axis=0, tiled=True)
     with jax.named_scope("queries"):
         queries = lax.all_gather(sent, "x", axis=0)
-    with jax.named_scope("opponents"):
-        chunks = keys.reshape(N_HALF, CHUNK, E)
-        chunks = exchange(jnp.concatenate([chunks, chunks]), BLOCK)
-        chosen = call(select_kernel, bf16(N_HALF, ROUNDS, CHUNK, E), plan, chunks, queries, specs=[smem, whole, anywhere])
-        others = exchange(chosen, HALF)
     with jax.named_scope("own"):
-        own_exps, match, own_sums = call(
+        own_exps, match, own_sums, plan = call(
             own_kernel,
-            (bf16(N_X * R, GATHERED), bf16(N_X * R, E), f32(16, E)),
+            (bf16(N_X * R, GATHERED), bf16(N_X * R, E), f32(16, E), jax.ShapeDtypeStruct(plan.shape, plan.dtype)),
             queries,
             keys,
+            plan,
             cost_estimate=cost(GATHERED),
         )
+    with jax.named_scope("opponents"):
+        chunks = jnp.broadcast_to(keys.reshape(N_HALF, CHUNK, E), (2, N_HALF, CHUNK, E))
+        chunks = exchange(chunks.reshape(N_BLOCK, CHUNK, E), BLOCK)
+        chosen = call(select_kernel, bf16(N_HALF, ROUNDS, CHUNK, E), plan, chunks, specs=[smem, whole])
+        others = exchange(chosen, HALF)
     with jax.named_scope("others"):
         exps, line = call(
             others_kernel,

time: 140 us -> 138 us (0.986)
  blocking collectives: 93 us -> 110 us
  waiting for transfers between devices: 13.8 us -> 0.74 us
  starting transfers between devices: 11.9 us -> 7.17 us
    all_to_all x3 -> x4, blocking collectives: 50.5 us -> 67.3 us  [exchange(): return lax.all_to_all(value, axes, 0, 0, tiled=True)]
    all_to_all x2 -> x1, waiting for transfers between devices: 13.8 us -> 0.74 us  [exchange(): return lax.all_to_all(value, axes, 0, 0, tiled=True)]
    all_to_all x2 -> x1, starting transfers between devices: 11.9 us -> 7.17 us  [exchange(): return lax.all_to_all(value, axes, 0, 0, tiled=True)]
    unnamed x12 -> x10, local copies, waits for them, and re-layouts: 2.75 us -> 2.82 us
  transfers between devices with their start and end apart: 2 -> 1, of which waited for: 2 -> 1; matrix products, arithmetic and copies ran while one was open for 0% -> 0% of each run, Pallas kernels for 3% -> 3%
where the time goes in v7:
time: 138 us
  blocking collectives  110 us (80%)
  Pallas kernels  15.6 us (11%)
  starting transfers between devices  7.17 us (5%)
  local copies, waits for them, and re-layouts  3.83 us (3%)
    all_to_all x4, blocking collectives, exchange(): return lax.all_to_all(value, axes, 0, 0, tiled=True)  67.3 us
    all_gather x1, blocking collectives, body(): keys = lax.all_gather(rounded, 'zh', axis=0, tiled=True)  29.4 us
    pallas_call x6, Pallas kernels, call(): pl.pallas_call(kernel, out_shape=out_shape, in_specs=specs or [whole] * l...  13.8 us
    all_gather x1, blocking collectives, body(): queries = lax.all_gather(sent, 'x', axis=0)  13.1 us
    all_to_all x1, starting transfers between devices, exchange(): return lax.all_to_all(value, axes, 0, 0, tiled=True)  7.17 us
    unnamed x10, local copies, waits for them, and re-layouts  2.82 us
  transfers between devices with their start and end apart: 1, of which 1 were waited for; matrix products, arithmetic and copies ran while one was open for 0% of the time, Pallas kernels for 3%

profile of v7, /device:TPU:32, one launch (start us, length us, event | category | flops | bytes accessed | tf_op | source)
XLA Modules:
  0.0 137.9 jit_solution(2781595787446872391)
XLA Ops:
  0.6 1.7 %normalize.1 = (bf16[384,128]{1,0:T(8,128)(2,1)}, bf16[400,128]{1,0:T(8,128)(2,1)}, s32[2,32]{1,0:T(2,128)}) custom-call(f32[384,128]{1,0:T(8,128)} %embed_ref.3, s32[3,128]{1,0:T(4,128)} %bitcast.11, s32[2,32]{1,0:T(2,128)} %plan_ref.1), custom_call_target="tpu_custom_call" | custom-call | tf_op jit(solution)/shard_map/normalize/pallas_call | solution.py:253
  2.4 29.4 %all_gather.11.keys_ref = bf16[1536,128]{1,0:T(8,128)(2,1)S(1)} all-gather(bf16[384,128]{1,0:T(8,128)(2,1)} %get-tuple-element.18), channel_id=1, replica_groups=mesh['zu'=2,'zl'=2,'y'=4,'c'=2,'x'=4,'zh'=4] {'zh'}, dimensions={0}, use_global_device_ids=true | all-gather | bytes 491520 | tf_op jit(solution)/shard_map/own/all_gather | solution.py:261
  31.8 1.0 broadcast_in_dim.3
  32.8 7.2 %all-to-all-start = ((bf16[32,96,128]{2,1,0:T(8,128)(2,1)}), bf16[32,96,128]{2,1,0:T(8,128)(2,1)S(1)}, u32[]{:S(2)}, u32[]{:S(2)}) async-start(bf16[32,96,128]{2,1,0:T(8,128)(2,1)} %bitcast.3), calls=%async_computation | async-start | bytes 1572864 | tf_op jit(solution)/shard_map/opponents/all_to_all | solution.py:230
  40.0 13.1 %all-gather = bf16[1600,128]{1,0:T(8,128)(2,1)S(1)} all-gather(bf16[400,128]{1,0:T(8,128)(2,1)} %get-tuple-element.17), channel_id=2, replica_groups=mesh['zu'=2,'zl'=2,'y'=4,'c'=2,'x'=4,'zh'=4] {'x'}, dimensions={0}, use_global_device_ids=true | all-gather | bytes 512000 | tf_op jit(solution)/shard_map/queries/all_gather | solution.py:263
  53.1 0.0 copy-start.2
  53.1 0.7 copy-done.2
  53.8 3.8 %own.1 = (bf16[1536,1536]{1,0:T(8,128)(2,1)S(1)}, bf16[1536,128]{1,0:T(8,128)(2,1)S(1)}, f32[16,128]{1,0:T(8,128)S(1)}, s32[2,32]{1,0:T(2,128)S(1)}) custom-call(bf16[4,400,128]{2,1,0:T(8,128)(2,1)S(1)} %bitcast.9, bf16[1536,128]{1,0:T(8,128)(2,1)S(1)} %all_gather.11.keys_ref, s32[2,32]{1,0:T(2,128)S(1)} %copy-done.2), custom_call_target="tpu_custom_call" | custom-call | flops 603979776 | bytes 4718592 | tf_op jit(solution)/shard_map/own/pallas_call | solution.py:234
  57.6 0.0 copy-start
  57.6 2.1 %copy-done = bf16[1536,1536]{1,0:T(8,128)(2,1)} copy-done((bf16[1536,1536]{1,0:T(8,128)(2,1)}, bf16[1536,1536]{1,0:T(8,128)(2,1)S(1)}, u32[]{:S(2)}) %copy-start) | copy-done | bytes 4718616
  59.7 0.7 all-to-all-done.chunks_ref
  60.4 0.6 opponents.1
  61.1 17.3 %all_to_all.25.keys_ref.far_ref = bf16[16,2,96,128]{3,2,1,0:T(8,128)(2,1)S(1)} all-to-all(bf16[16,2,96,128]{3,2,1,0:T(8,128)(2,1)S(1)} %opponents.1), channel_id=1, replica_groups=mesh['zu'=2,'zl'=2,'y'=4,'c'=2,'x'=4,'zh'=4] {'zl','y','c'}, dimensions={0} | all-to-all | bytes 1572864 | tf_op jit(solution)/shard_map/opponents/all_to_all | solution.py:230
  78.4 2.9 %others.1 = (bf16[1536,3072]{1,0:T(8,128)(2,1)S(1)}, f32[32,16,128]{2,1,0:T(8,128)S(1)}) custom-call(bf16[4,400,128]{2,1,0:T(8,128)(2,1)S(1)} %bitcast.10, bf16[16,2,96,128]{3,2,1,0:T(8,128)(2,1)S(1)} %all_to_all.25.keys_ref.far_ref, f32[16,128]{1,0:T(8,128)S(1)} %get-tuple-element.22.own_ref), custom_call_target="tpu_custom_call" | custom-call | flops 1207959552 | bytes 9437184 | tf_op jit(solution)/shard_map/others/pallas_call | solution.py:234
  81.2 0.0 copy-start.1
  81.3 14.3 %all_to_all.26.line_ref = f32[32,16,128]{2,1,0:T(8,128)S(1)} all-to-all(f32[32,16,128]{2,1,0:T(8,128)S(1)} %get-tuple-element.25), channel_id=1, replica_groups=mesh['zu'=2,'zl'=2,'y'=4,'c'=2,'x'=4,'zh'=4] {'c','y','x'}, dimensions={0} | all-to-all | bytes 524288 | tf_op jit(solution)/shard_map/sums/all_to_all | solution.py:230
  95.6 0.6 sums.1
  96.2 21.8 %all_to_all.27.sums_ref = bf16[16,32,128]{2,1,0:T(8,128)(2,1)S(1)} all-to-all(bf16[16,32,128]{2,1,0:T(8,128)(2,1)S(1)} %get-tuple-element.27), channel_id=1, replica_groups=mesh['zu'=2,'zl'=2,'y'=4,'c'=2,'x'=4,'zh'=4] {'zu','zl','zh'}, dimensions={0} | all-to-all | bytes 262144 | tf_op jit(solution)/shard_map/sums/all_to_all | solution.py:230
  118.0 0.0 slice-done
  118.0 0.0 slice-done.1
  118.0 5.1 %direction.1 = (f32[4,384,128]{2,1,0:T(8,128)S(1)}, f32[1,1]{1,0:T(1,128)}) custom-call(s32[2,32]{1,0:T(2,128)S(1)} %get-tuple-element.20.plan_ref, bf16[1536,1536]{1,0:T(8,128)(2,1)S(1)} %bitcast.7, bf16[1536,3072]{1,0:T(8,128)(2,1)S(1)} %get-tuple-element.23.others_ref, bf16[1536,128]{1,0:T(8,128)(2,1)S(1)} %all_gather.11.keys_ref, ...), custom_call_target="tpu_custom_call" | custom-call | flops 1811939328 | bytes 14155776 | tf_op jit(solution)/shard_map/direction/pallas_call | solution.py:234
  123.1 13.9 %all_to_all.28.parts_ref = f32[4,384,128]{2,1,0:T(8,128)S(1)} all-to-all(f32[4,384,128]{2,1,0:T(8,128)S(1)} %get-tuple-element.28), channel_id=1, replica_groups=mesh['zu'=2,'zl'=2,'y'=4,'c'=2,'x'=4,'zh'=4] {'x'}, dimensions={0} | all-to-all | bytes 1572864 | tf_op jit(solution)/shard_map/direction/all_to_all | solution.py:230
  137.0 0.0 copy-done.1
  137.0 0.9 finish.1
  (3 shorter events, 0.0 us)
Async XLA Ops:
  32.8 27.6 %all-to-all-start = ((bf16[32,96,128]{2,1,0:T(8,128)(2,1)}), bf16[32,96,128]{2,1,0:T(8,128)(2,1)S(1)}, u32[]{:S(2)}, u32[]{:S(2)}) async-start(bf16[32,96,128]{2,1,0:T(8,128)(2,1)} %bitcast.3), calls=%async_computation | async-start | bytes 1572864 | tf_op jit(solution)/shard_map/opponents/all_to_all | solution.py:230
  53.1 0.7 copy-start.2
  57.6 2.1 %copy-start = (bf16[1536,1536]{1,0:T(8,128)(2,1)}, bf16[1536,1536]{1,0:T(8,128)(2,1)S(1)}, u32[]{:S(2)}) copy-start(bf16[1536,1536]{1,0:T(8,128)(2,1)S(1)} %get-tuple-element.21.own_ref) | copy-start | bytes 14155780
  60.4 57.6 %slice-start = ((s8[4718592]{0:T(1024)(128)(4,1)}), s8[4194304]{0:T(1024)(128)(4,1)S(1)}, s32[]{:S(2)}) async-start(s8[4718592]{0:T(1024)(128)(4,1)} %bitcast.6), calls=%async_computation.5 | async-start | bytes 8388608
  78.4 39.7 %slice-start.1 = ((s8[4718592]{0:T(1024)(128)(4,1)}), s8[524288]{0:T(1024)(128)(4,1)S(1)}, s32[]{:S(2)}) async-start(s8[4718592]{0:T(1024)(128)(4,1)} %bitcast.6), calls=%async_computation.6 | async-start | bytes 1048576
  81.2 55.7 %copy-start.1 = (f32[384,128]{1,0:T(8,128)S(1)}, f32[384,128]{1,0:T(8,128)}, u32[]{:S(2)}) copy-start(f32[384,128]{1,0:T(8,128)} %embed_ref.3) | copy-start | bytes 589828
